TPU v7x, 32 devices: a whole 2x2x4 slice. The times are simulated.
32 devices in a mesh: dp: 4 (over z), ctx: 8 (over y, x, core).
Axes of the slice: x: 2, y: 2, z: 4, core: 2. Of those that a mesh axis runs over, the one named last changes fastest.
Arguments:
- queries: bfloat16 [4, 1024, 1024], P('dp', 'ctx'), may hold values from -6 to 6
- key_in: bfloat16 [4, 1024, 1024], P('dp', 'ctx'), may hold values from -6 to 6
- value_in: bfloat16 [4, 1024, 2048], P('dp', 'ctx'), may hold values from -6 to 6
- gate_in: bfloat16 [4, 1024, 2048], P('dp', 'ctx'), may hold values from -6 to 6
- residual_in: bfloat16 [4, 1024, 2048], P('dp', 'ctx'), may hold values from -6 to 6
- log_decay: float32 [4, 16, 1024], P('dp', None, 'ctx'), may hold values from -1 to 0
- beta_logit: float32 [4, 16, 1024], P('dp', None, 'ctx'), may hold values from -6 to 6
- lengths: int32 [4, 4], P('dp'), may hold values from 1 to 512, 1024 in all within a row
- head_gain: float32 [128], replicated, may hold values from 0.1 to 1.9
- out_proj: bfloat16 [2048, 2048], replicated, may hold values from -0.125 to 0.125
- post_gain: float32 [2048], replicated, may hold values from 0.1 to 1.9
- expert_in: bfloat16 [64, 2048, 1024], P(('dp', 'ctx')), may hold values from -0.125 to 0.125
- expert_out: bfloat16 [64, 512, 2048], P(('dp', 'ctx')), may hold values from -0.25 to 0.25
- routes: int32 [4, 1024, 10], P('dp', 'ctx'), may hold values from 0 to 63, all different within a row; in each aligned block of 128 rows (0 to 127, 128 to 255, ..., all dimensions but the last counted through in order) at most 24 rows name the same one
- route_gates: float32 [4, 1024, 10], P('dp', 'ctx'), may hold values from 0.05 to 0.25
Outputs:
- layer_out: bfloat16 [4, 1024, 2048], P('dp', 'ctx')
Inputs may be any that keep to these rules, and one draw needn't show every extreme that they name: `routes`: each row names 10 different experts; among the rows of one device (aligned blocks of 128 positions) no expert is named more than 24 times, a bound that some block reaches. The lengths of a pack sum to 1024.
All inputs are finite; a program needn't handle non-finite values.
Results may differ from a plain program's by a relative error of at most 0.014.
Values may be sent and summed in bfloat16 or wider, within the bound.
A program may use at most 256 MiB of HBM per device.

v0:
```python
import jax
import jax.numpy as jnp
from jax import lax
from jax.sharding import PartitionSpec as P

D = 2048
DK = 128
DV = 128
FF = 512
TOPK = 10
HK = 8
HV = 16
BLOCK = 64


EPSILON = 1e-06
HIGHEST = lax.Precision.HIGHEST
ROWWISE = lax.Precision.HIGH


def entering(part, axis, combine, identity):
    place = lax.axis_index(axis)
    gathered = jax.tree.map(lambda a: lax.all_gather(a, axis), part)
    state = jax.tree.map(lambda a, e: jnp.zeros_like(a) + jnp.asarray(e, a.dtype), part, identity)

    def one(lap, state):
        return combine(
            state, jax.tree.map(lambda a: lax.dynamic_index_in_dim(a, lap, 0, False), gathered)
        )

    return lax.fori_loop(0, place, one, state)


def unit_heads(matrix, head_count, factor):
    shaped = matrix.astype(jnp.float32).reshape(matrix.shape[0], head_count, -1)
    return shaped * lax.rsqrt(jnp.sum(shaped * shaped, -1, keepdims=True) + EPSILON) * factor


def segment_of(lengths, positions):
    starts = jnp.cumsum(lengths) - lengths
    return jnp.sum((starts[:, None] <= positions[None, :]).astype(jnp.int32), 0) - 1


def block_terms(queries, key_rows, value_rows, beta_gate, decay_log, segment, seg_before):
    length = key_rows.shape[1]
    cumulative = jnp.cumsum(decay_log, axis=-1)
    rows_at = jnp.arange(length)[:, None]
    cols_at = jnp.arange(length)[None, :]
    same_doc = (segment[:, None] == segment[None, :]) & (rows_at >= cols_at)
    log_gap = jnp.minimum(cumulative[:, :, None] - cumulative[:, None, :], 0.0)
    decay_pair = jnp.where(same_doc[None], jnp.exp(log_gap), 0.0)
    from_start = jnp.where((segment == seg_before)[None, :], jnp.exp(cumulative), 0.0)
    to_end = decay_pair[:, -1, :]
    key_inner = jnp.einsum("hcd,hsd->hcs", key_rows, key_rows, precision=ROWWISE)
    lower_part = jnp.where(
        (rows_at > cols_at)[None], beta_gate[:, :, None] * decay_pair * key_inner, 0.0
    )
    system = jnp.eye(length, dtype=jnp.float32)[None] + lower_part
    right_side = jnp.concatenate(
        [beta_gate[:, :, None] * value_rows, (beta_gate * from_start)[:, :, None] * key_rows],
        axis=-1,
    )
    solved = jax.scipy.linalg.solve_triangular(system, right_side, lower=True, unit_diagonal=True)
    value_width = value_rows.shape[-1]
    pseudo = solved[..., :value_width]
    weights = solved[..., value_width:]
    scores = jnp.einsum("hcd,hsd->hcs", queries, key_rows, precision=ROWWISE) * decay_pair
    weighted = key_rows * to_end[:, :, None]
    key_width = key_rows.shape[-1]
    transition = from_start[:, -1][:, None, None] * jnp.eye(key_width, dtype=jnp.float32)[
        None
    ] - jnp.einsum("hcd,hce->hde", weighted, weights, precision=HIGHEST)
    offset = jnp.einsum("hcd,hce->hde", weighted, pseudo, precision=HIGHEST)
    return (pseudo, weights, scores, from_start, transition, offset)


def block_output(queries, pseudo, weights, scores, from_start, carried):
    errors = pseudo - jnp.einsum("hcd,hde->hce", weights, carried, precision=ROWWISE)
    return jnp.einsum(
        "hcd,hde->hce", queries * from_start[:, :, None], carried, precision=ROWWISE
    ) + jnp.einsum("hcs,hse->hce", scores, errors, precision=ROWWISE)


def apply_map(transition, carried):
    return jnp.einsum("hde,hef->hdf", transition, carried, precision=HIGHEST)


def head_blocks(matrix, block_len):
    length, head_count, inner_width = matrix.shape
    return matrix.reshape(length // block_len, block_len, head_count, inner_width).transpose(
        0, 2, 1, 3
    )


def prepare(queries, key_in, value_in, log_decay, beta_logit, segment, seg_before):
    length = queries.shape[0]
    group_size = HV // HK
    query_heads = jnp.repeat(unit_heads(queries, HK, DK ** (-0.5)), group_size, axis=1)
    key_heads = jnp.repeat(unit_heads(key_in, HK, 1.0), group_size, axis=1)
    value_heads = value_in.astype(jnp.float32).reshape(length, HV, DV)
    nblock = length // BLOCK
    beta_gate = jax.nn.sigmoid(beta_logit).reshape(HV, nblock, BLOCK).transpose(1, 0, 2)
    decay_log = log_decay.reshape(HV, nblock, BLOCK).transpose(1, 0, 2)
    seg_blocks = segment.reshape(nblock, BLOCK)
    seg_starts = jnp.concatenate([jnp.reshape(seg_before, (1,)), seg_blocks[:-1, -1]])
    query_blocks = head_blocks(query_heads, BLOCK)
    terms = jax.vmap(block_terms)(
        query_blocks,
        head_blocks(key_heads, BLOCK),
        head_blocks(value_heads, BLOCK),
        beta_gate,
        decay_log,
        seg_blocks,
        seg_starts,
    )
    return (query_blocks, terms)


def finish(query_blocks, terms, start_state, gate_in, residual_in, head_gain, out_proj):
    pseudo, weights, scores, from_start, transition, offset = terms

    def advance(carried, member):
        return (apply_map(member[0], carried) + member[1], carried)

    final_state, block_starts = lax.scan(advance, start_state, (transition, offset))
    outputs = jax.vmap(block_output)(
        query_blocks, pseudo, weights, scores, from_start, block_starts
    )
    length = gate_in.shape[0]
    outputs = outputs.transpose(0, 2, 1, 3).reshape(length, HV, DV)
    mean_square = jnp.mean(outputs * outputs, -1, keepdims=True)
    gate_heads = gate_in.astype(jnp.float32).reshape(length, HV, DV)
    normed = (
        (outputs * lax.rsqrt(mean_square + EPSILON) * head_gain * jax.nn.silu(gate_heads))
        .reshape(length, HV * DV)
        .astype(jnp.bfloat16)
    )
    mixed = jnp.dot(normed, out_proj, preferred_element_type=jnp.float32)
    return (residual_in.astype(jnp.float32) + mixed).astype(jnp.bfloat16)


def post_norm(hidden_state, post_gain):
    widened = hidden_state.astype(jnp.float32)
    return (
        widened * lax.rsqrt(jnp.mean(widened * widened, -1, keepdims=True) + EPSILON) * post_gain
    ).astype(jnp.bfloat16)


def rank_of(flat_ids, experts):
    onehot = (flat_ids[:, None] == jnp.arange(experts, dtype=jnp.int32)[None, :]).astype(jnp.int32)
    return jnp.sum((jnp.cumsum(onehot, 0) - onehot) * onehot, 1)


def expert_apply(routed, expert_in, expert_out):
    gate_up = jnp.einsum("sjcd,jdf->sjcf", routed, expert_in, preferred_element_type=jnp.float32)
    hidden_units = (jax.nn.silu(gate_up[..., :FF]) * gate_up[..., FF:]).astype(jnp.bfloat16)
    return jnp.einsum(
        "sjcf,jfd->sjcd", hidden_units, expert_out, preferred_element_type=jnp.float32
    ).astype(jnp.bfloat16)


def per_device(
    queries,
    key_in,
    value_in,
    gate_in,
    residual_in,
    log_decay,
    beta_logit,
    lengths,
    head_gain,
    out_proj,
    post_gain,
    expert_in,
    expert_out,
    routes,
    route_gates,
):
    tokens_dev = queries.shape[1]
    ctx_index = lax.axis_index("ctx")
    positions = ctx_index * tokens_dev + jnp.arange(tokens_dev, dtype=jnp.int32)
    segment = segment_of(lengths[0], positions)
    previous = segment_of(lengths[0], jnp.reshape(positions[0] - 1, (1,)))[0]
    seg_before = jnp.where(ctx_index > 0, previous, -1)
    query_blocks, terms = prepare(
        queries[0], key_in[0], value_in[0], log_decay[0], beta_logit[0], segment, seg_before
    )
    eye_maps = jnp.broadcast_to(jnp.eye(DK, dtype=jnp.float32), (HV, DK, DK))
    zero_offset = jnp.zeros((HV, DK, DV), jnp.float32)

    def compose(carry_pair, member):
        return (
            (apply_map(member[0], carry_pair[0]), apply_map(member[0], carry_pair[1]) + member[1]),
            None,
        )

    device_pair, unused = lax.scan(compose, (eye_maps, zero_offset), (terms[4], terms[5]))

    def combine(earlier, later):
        return (apply_map(later[0], earlier[0]), apply_map(later[0], earlier[1]) + later[1])

    prefix_map, prefix_offset = entering(
        (device_pair[0], device_pair[1]), "ctx", combine, (eye_maps, zero_offset)
    )
    hidden_state = finish(
        query_blocks, terms, prefix_offset, gate_in[0], residual_in[0], head_gain, out_proj
    )
    expert_input = post_norm(hidden_state, post_gain)
    local_experts = expert_in.shape[0]
    device_count = lax.axis_size("dp") * lax.axis_size("ctx")
    experts_all = local_experts * device_count
    capacity = tokens_dev * TOPK * 6 // (5 * experts_all)
    flat_ids = routes[0].reshape(-1)
    slot_rank = rank_of(flat_ids, experts_all)
    outbound = (
        jnp.zeros((experts_all, capacity, D), jnp.bfloat16)
        .at[flat_ids, slot_rank]
        .set(jnp.repeat(expert_input, TOPK, axis=0))
    )
    outbound = outbound.reshape(device_count, local_experts, capacity, D)
    computed = expert_apply(
        lax.all_to_all(outbound, ("dp", "ctx"), split_axis=0, concat_axis=0, tiled=True),
        expert_in,
        expert_out,
    )
    returned = lax.all_to_all(computed, ("dp", "ctx"), split_axis=0, concat_axis=0, tiled=True)
    back_rows = returned.reshape(experts_all, capacity, D)[flat_ids, slot_rank]
    expert_mix = jnp.sum(
        back_rows.astype(jnp.float32).reshape(tokens_dev, TOPK, D) * route_gates[0][:, :, None], 1
    )
    summed = hidden_state.astype(jnp.float32) + expert_mix
    return summed.astype(jnp.bfloat16)[None]


def solution(mesh):
    in_specs = (
        P("dp", "ctx", None),
        P("dp", "ctx", None),
        P("dp", "ctx", None),
        P("dp", "ctx", None),
        P("dp", "ctx", None),
        P("dp", None, "ctx"),
        P("dp", None, "ctx"),
        P("dp", None),
        P(),
        P(),
        P(),
        P(("dp", "ctx"), None, None),
        P(("dp", "ctx"), None, None),
        P("dp", "ctx", None),
        P("dp", "ctx", None),
    )
    out_specs = P("dp", "ctx", None)
    return jax.shard_map(
        per_device, mesh=mesh, in_specs=in_specs, out_specs=out_specs, check_vma=False
    )
```

profile of v0, /device:TPU:0, one launch (start us, length us, event | category | flops | bytes accessed | tf_op | source)
XLA Modules:
  0.0 746.1 jit_solution(12715265910680456099)
XLA Ops:
  19.6 158.2 %custom-call.4 = f32[2,16,1,64,64]{3,4,2,1,0:T(8,128)S(1)} custom-call(f32[2,16,1,64,64]{4,3,2,1,0:T(8,128)} %fusion.42), custom_call_target="InvertDiagBlocksLowerTriangular" | custom-call | tf_op jit(solution)/shard_map/vmap(jit(_solve_triangular))/vmap()/triangular_solve | solution.py:63
  181.5 5.1 fusion.55
  186.6 4.0 multiply_subtract_fusion
  190.7 12.2 %while.39 = (s32[]{:T(128)}, f32[16,128,128]{2,1,0:T(8,128)S(1)}, f32[16,128,128]{2,1,0:T(8,128)}, f32[2,16,128,128]{3,2,1,0:T(8,128)S(1)}, f32[2,16,128,128]{3,2,1,0:T(8,128)}, /*index=5*/s32[]{:T(128)}, s32[]{:T(128)}) while((s32[]{:T(128)}, f32[16,128,128]{2,1,0:T(8,128)S(1)}, f32[16,128,128]{2,1,0:T(8,128)}, ...), condition=%wide.region_7.8_spmd.clone, body=%wide.region_6.7_spmd.clone.sunk | while | flops 805830656 | bytes 11535451 | solution.py:197
  192.2 3.4 convolution_add_fusion.10
  198.2 3.4 convolution_add_fusion.10
  207.7 34.5 %reduce-window.11 = s32[64,10,128]{2,1,0:T(8,128)} reduce-window(s32[64,10,128]{2,1,0:T(8,128)} %fusion.70, s32[]{:T(128)} %copy.184), window={size=1x1x128 pad=0_0x0_0x127_0}, to_apply=%region_13.14 | reduce-window | flops 10403840 | bytes 655364 | tf_op jit(solution)/shard_map/reduce-window.1
  251.5 9.7 %all-gather.5.cloned.1.call-done = f32[128,128,128]{2,1,0:T(8,128)} async-done(((f32[16,128,128]{2,1,0:T(8,128)}), f32[128,128,128]{2,1,0:T(8,128)}) %all-gather.5.cloned.1.call-update) | async-done | bytes 8388624 | tf_op jit(solution)/shard_map/all_gather | solution.py:23
  261.2 56.3 %all-gather.7.cloned.1.call-done = f32[128,128,128]{2,1,0:T(8,128)} async-done(((f32[16,128,128]{2,1,0:T(8,128)}), f32[128,128,128]{2,1,0:T(8,128)}) %all-gather.7.cloned.1.call-update) | async-done | bytes 8388624 | tf_op jit(solution)/shard_map/all_gather | solution.py:23
  317.6 6.9 while.38
  324.6 3.3 convolution_subtract_fusion
  331.0 5.5 multiply_reduce_fusion.1
  336.6 4.4 broadcast_in_dim.62
  341.0 9.8 %reshape.297 = bf16[1280,2048]{1,0:T(8,128)(2,1)} reshape(bf16[128,10,2048]{2,1,0:T(8,128)(2,1)} %broadcast_in_dim.62) | data formatting | bytes 10485760 | tf_op jit(solution)/shard_map/reshape | solution.py:218
  350.9 14.7 %scatter_custom_fusion = bf16[1536,2048]{1,0:T(8,128)(2,1)} fusion(s32[1280]{0:T(1024)S(1)} %broadcast_select_fusion, bf16[1280,2048]{1,0:T(8,128)(2,1)} %reshape.297, bf16[]{:T(256)} %constant.92.clone.1), kind=kCustom, calls=%fused_computation.31 | custom fusion | bytes 6291968
  365.6 163.2 %all_to_all.10 = bf16[32,2,24,2048]{3,2,1,0:T(8,128)(2,1)S(1)} all-to-all(bf16[32,2,24,2048]{3,2,1,0:T(8,128)(2,1)} %bitcast.187), channel_id=1, replica_groups=mesh['dp'=4,'ctx'=8] {'dp','ctx'}, dimensions={0} | all-to-all | bytes 12582912 | tf_op jit(solution)/shard_map/all_to_all | solution.py:222
  528.8 10.9 %fusion.24 = f32[32,2,24,1024]{3,2,0,1:T(8,128)} fusion(bf16[2,2048,1024]{2,1,0:T(8,128)(2,1)} %param.32, bf16[32,2,24,2048]{3,2,1,0:T(8,128)(2,1)S(1)} %all_to_all.10), kind=kOutput, calls=%fused_computation.33 | convolution fusion | flops 6442450944 | bytes 20971520 | tf_op jit(solution)/shard_map/sjcd,jdf->sjcf/dot_general | solution.py:155
  539.8 6.9 convert_bitcast_fusion
  546.6 3.2 copy.96
  549.9 4.1 all-to-all-start.1
  554.1 139.9 %all-to-all-done.1 = bf16[32,2,24,2048]{3,2,1,0:T(8,128)(2,1)} async-done(((bf16[32,2,24,2048]{3,2,1,0:T(8,128)(2,1)}), bf16[32,2,24,2048]{3,2,1,0:T(8,128)(2,1)}, u32[]{:S(2)}, u32[]{:S(2)}) %all-to-all-start.1) | async-done | bytes 6291488 | tf_op jit(solution)/shard_map/all_to_all | solution.py:226
  693.9 24.2 %gather_fusion = bf16[1280,2048]{1,0:T(8,128)(2,1)} fusion(bf16[64,24,2048]{2,1,0:T(8,128)(2,1)} %bitcast.39, s32[1280]{0:T(1024)S(1)} %get-tuple-element.156), kind=kCustom, calls=%fused_computation | custom fusion | bytes 10496000 | tf_op jit(solution)/shard_map/gather | solution.py:227
  718.1 10.4 %reshape.287 = f32[128,10,2048]{2,1,0:T(8,128)} reshape(bf16[1280,2048]{1,0:T(8,128)(2,1)} %gather_fusion) | data formatting | bytes 15728640 | tf_op jit(solution)/shard_map/convert_element_type | solution.py:229
  728.5 9.6 %multiply_reduce_fusion = f32[128,2048]{1,0:T(8,128)S(1)} fusion(f32[128,10,2048]{2,1,0:T(8,128)} %reshape.287, f32[128,10]{1,0:T(8,128)S(1)} %bitcast.198), kind=kLoop, calls=%fused_computation.23 | loop fusion | flops 4980736 | bytes 11539456 | tf_op jit(solution)/shard_map/reduce_sum | solution.py:228
  (138 shorter events, 45.6 us)
Async XLA Ops:
  6.5 240.8 %copy-start = (f32[128]{0:T(128)S(1)}, f32[128]{0:T(128)}, u32[]{:S(2)}) copy-start(f32[128]{0:T(128)} %param.29) | copy-start | bytes 1540
  6.5 8.6 %copy-start.11 = (bf16[1,128,2048]{2,1,0:T(8,128)(2,1)S(1)}, bf16[1,128,2048]{2,1,0:T(8,128)(2,1)}, u32[]{:S(2)}) copy-start(bf16[1,128,2048]{2,1,0:T(8,128)(2,1)} %param.23) | copy-start | bytes 1572868
  6.5 254.7 %all-gather.5.cloned.1.call-start = ((), (), s32[]{:S(2)}) async-start(), calls=%async_computation.2 | async-start | bytes 9437184 | tf_op jit(solution)/shard_map/all_gather | solution.py:23
  17.5 169.1 %copy-start.4 = (f32[128,8,2,128]{3,0,2,1:T(8,128)}, f32[128,8,2,128]{3,0,2,1:T(8,128)S(1)}, u32[]{:S(2)}) copy-start(f32[128,8,2,128]{3,0,2,1:T(8,128)S(1)} %broadcast_in_dim.57) | copy-start | bytes 3145732
  181.5 9.1 %copy-start.6 = (f32[2,16,64,256]{3,2,1,0:T(8,128)}, f32[2,16,64,256]{3,2,1,0:T(8,128)S(1)}, u32[]{:S(2)}) copy-start(f32[2,16,64,256]{3,2,1,0:T(8,128)S(1)} %fusion.31) | copy-start | bytes 6291460
  190.7 14.0 %copy-start.14 = (s32[1,128,10]{1,0,2:T(1,128)S(1)}, s32[1,128,10]{1,0,2:T(1,128)}, u32[]{:S(2)}) copy-start(s32[1,128,10]{1,0,2:T(1,128)} %param.34) | copy-start | bytes 15364
  190.7 14.6 %copy-start.12 = (bf16[1,128,1024]{2,1,0:T(8,128)(2,1)S(1)}, bf16[1,128,1024]{2,1,0:T(8,128)(2,1)}, u32[]{:S(2)}) copy-start(bf16[1,128,1024]{2,1,0:T(8,128)(2,1)} %param.21) | copy-start | bytes 786436
  204.0 113.6 %all-gather.7.cloned.1.call-start = ((), (), s32[]{:S(2)}) async-start(), calls=%async_computation.3 | async-start | bytes 9437184 | tf_op jit(solution)/shard_map/all_gather | solution.py:23
  205.3 41.8 %copy-start.17 = (s32[2]{0:T(128)S(1)}, s32[2]{0:T(128)}, u32[]{:S(2)}) copy-start(s32[2]{0:T(128)} %constant.108) | copy-start | bytes 28
  205.3 41.9 %copy-start.16 = (s32[2]{0:T(128)S(1)}, s32[2]{0:T(128)}, u32[]{:S(2)}) copy-start(s32[2]{0:T(128)} %constant.111) | copy-start | bytes 28
  205.7 43.8 %copy-start.5 = (f32[128,8,2,128]{3,0,2,1:T(8,128)S(1)}, f32[128,8,2,128]{3,0,2,1:T(8,128)}, u32[]{:S(2)}) copy-start(f32[128,8,2,128]{3,0,2,1:T(8,128)} %copy-done.4) | copy-start | bytes 3145732
  248.5 1.0 copy-start.7
  318.1 2.0 copy-start.2
  321.3 2.0 copy-start.2
  324.5 3.3 copy-start.8
  324.5 3.3 copy-start.9
  324.5 4.4 copy-start.10
  328.9 2.0 copy-start.19
  328.9 2.0 copy-start.20
  331.0 5.5 copy-start.13
  528.8 10.9 %copy-start.18 = (bf16[2,512,2048]{2,1,0:T(8,128)(2,1)S(1)}, bf16[2,512,2048]{2,1,0:T(8,128)(2,1)}, u32[]{:S(2)}) copy-start(bf16[2,512,2048]{2,1,0:T(8,128)(2,1)} %param.33) | copy-start | bytes 12582916
  549.9 4.1 copy-start.15
  549.9 144.1 %all-to-all-start.1 = ((bf16[32,2,24,2048]{3,2,1,0:T(8,128)(2,1)}), bf16[32,2,24,2048]{3,2,1,0:T(8,128)(2,1)}, u32[]{:S(2)}, u32[]{:S(2)}) async-start(bf16[32,2,24,2048]{3,2,1,0:T(8,128)(2,1)} %copy.96), calls=%async_computation.1 | async-start | bytes 12582912 | tf_op jit(solution)/shard_map/all_to_all | solution.py:226
  728.5 10.5 %copy-start.1 = (f32[128]{0:T(128)S(1)}, f32[128]{0:T(128)}, u32[]{:S(2)}) copy-start(f32[128]{0:T(128)} %param.29) | copy-start | bytes 1540
  (1 other events, 1.0 us)
Sparse Core Ops, SparseCore 0:
  204.1 57.0 all-gather.4
  263.1 54.3 all-gather.6
where the time goes:
time: 754 us; the launch traced here: 746 us
  other arithmetic  215 us (29%)
  waiting for transfers between devices  207 us (27%)
  blocking collectives  163 us (22%)
  local copies, waits for them, and re-layouts  86 us (11%)
  matrix products  55.3 us (7%)
  between operations  14.9 us (2%)
    all_to_all x1, blocking collectives, per_device(): lax.all_to_all(outbound, ('dp', 'ctx'), split_axis=0, concat_axis=0, tile...  163 us
    another operation x2, other arithmetic, block_terms(): jax.scipy.linalg.solve_triangular(system, right_side, lower=True, unit_di...  158 us
    all_to_all x1, waiting for transfers between devices, per_device(): lax.all_to_all(computed, ('dp', 'ctx'), split_axis=0, concat_axis=0, tile...  140 us
    all_gather x2, waiting for transfers between devices, entering(): gathered = jax.tree.map(lambda a: lax.all_gather(a, axis), part)  66 us
    another operation x4, other arithmetic  36.7 us
    gather x1, local copies, waits for them, and re-layouts, per_device(): back_rows = returned.reshape(experts_all, capacity, D)[flat_ids, slot_rank]  24.2 us
    unnamed x45, local copies, waits for them, and re-layouts  17.3 us
  transfers between devices with their start and end apart: 3, of which 3 were waited for; matrix products, arithmetic and copies ran while one was open for 6% of the time, Pallas kernels for 0%

commit v1 on v0

--- a/solution.py
+++ b/solution.py
@@ -1,6 +1,8 @@
 import jax
 import jax.numpy as jnp
 from jax import lax
+from jax.experimental import pallas as pl
+from jax.experimental.pallas import tpu as pltpu
 from jax.sharding import PartitionSpec as P
 
 D = 2048
@@ -159,7 +161,7 @@
     ).astype(jnp.bfloat16)
 
 
-def per_device(
+def per_device_long(
     queries,
     key_in,
     value_in,
@@ -232,6 +234,297 @@
     return summed.astype(jnp.bfloat16)[None]
 
 
+TILE = 128
+SCAL = 128
+BF = jnp.bfloat16
+F32 = jnp.float32
+
+
+def mm(a, b):
+    return jnp.dot(a, b, preferred_element_type=F32)
+
+
+def mm_nt(a, b):
+    return lax.dot_general(a, b, (((1,), (1,)), ((), ())), preferred_element_type=F32)
+
+
+def halves(a):
+    high = a.astype(BF)
+    return high, (a - high.astype(F32)).astype(BF)
+
+
+def dot3(a, b):
+    ah, al = a
+    bh, bl = b
+    return mm(ah, bh) + (mm(ah, bl) + mm(al, bh))
+
+
+def mixer_kernel(lengths_ref, x_ref, gain_ref, out_ref, pseudo, weights, scores, keyed, ends):
+    total = x_ref.shape[0]
+    tiles = total // TILE
+    group = HV // HK
+    rows = lax.broadcasted_iota(jnp.int32, (TILE, TILE), 0)
+    cols = lax.broadcasted_iota(jnp.int32, (TILE, TILE), 1)
+    eye = (rows == cols).astype(F32)
+    tri = (rows >= cols).astype(BF)
+    starts = []
+    at = jnp.int32(0)
+    for j in range(lengths_ref.shape[1]):
+        starts.append(at)
+        at = at + lengths_ref[0, j]
+
+    def segment(pos):
+        seg = jnp.zeros(pos.shape, jnp.int32)
+        for start in starts:
+            seg = seg + (start <= pos).astype(jnp.int32)
+        return seg
+
+    def terms_of(tile):
+        base = pl.multiple_of(tile * TILE, TILE)
+        q = x_ref[pl.ds(base, TILE), 0:DK]
+        k = x_ref[pl.ds(base, TILE), DK : 2 * DK]
+        sc = x_ref[pl.ds(base, TILE), 2 * DK + group * DV : 2 * DK + group * DV + SCAL]
+        cum = mm(tri, sc)
+        qf = q.astype(F32)
+        kf = k.astype(F32)
+        rq = lax.rsqrt(jnp.sum(qf * qf, -1, keepdims=True) + EPSILON) * DK ** (-0.5)
+        rk = lax.rsqrt(jnp.sum(kf * kf, -1, keepdims=True) + EPSILON)
+        scf = sc.astype(F32)
+        seg_c = segment(base + rows)
+        seg_r = segment(base + cols)
+        seg_b = segment(jnp.full((TILE, 1), base - 1, jnp.int32))
+        causal = (seg_c == seg_r) & (rows >= cols)
+        open_c = (seg_c[:, :1] == seg_b) & (base > 0)
+        g_c, beta_c, from_c = [], [], []
+        for h in range(group):
+            g = cum[:, h : h + 1] + cum[:, group + h : group + h + 1]
+            b = (
+                scf[:, 2 * group + h : 2 * group + h + 1]
+                + scf[:, 3 * group + h : 3 * group + h + 1]
+            )
+            g_c.append(g)
+            beta_c.append(b)
+            from_c.append(jnp.where(open_c, jnp.exp(g), 0.0))
+        packed = jnp.zeros((TILE, TILE), F32)
+        for n, col in enumerate(g_c + beta_c + from_c + [rk]):
+            packed = jnp.where(cols == n, col, packed)
+        flat = packed.T
+        rk_r = flat[3 * group : 3 * group + 1, :]
+        kk = mm_nt(k, k) * rk * rk_r
+        qk = mm_nt(q, k) * rq * rk_r
+        per_head = []
+        for h in range(group):
+            g_r = flat[h : h + 1, :]
+            beta_r = flat[group + h : group + h + 1, :]
+            from_r = flat[2 * group + h : 2 * group + h + 1, :]
+            pair = jnp.where(causal, jnp.exp(jnp.minimum(g_c[h] - g_r, 0.0)), 0.0)
+            lower = jnp.where(rows > cols, beta_c[h] * pair * kk, 0.0)
+            last = jnp.where(
+                (seg_c[TILE - 1 :, :1] == seg_c[:, :1]),
+                jnp.exp(jnp.minimum(g_c[h][TILE - 1 :, :] - g_c[h], 0.0)),
+                0.0,
+            )
+            per_head.append(
+                dict(
+                    tile=tile,
+                    h=h,
+                    base=base,
+                    lower=lower,
+                    score=qk * pair,
+                    beta_r=beta_r,
+                    scale_r=beta_r * from_r * rk_r,
+                    k=k,
+                    to_end=last * rk,
+                    read=from_c[h] * rq,
+                    from_end=from_c[h][TILE - 1 :, :],
+                )
+            )
+        return per_head
+
+    def build(step, carry):
+        work = []
+        for u in range(2):
+            work += terms_of(step * 2 + u)
+        near = ((rows ^ cols) == 1) & (rows > cols)
+        inverse = [eye - jnp.where(near, w["lower"], 0.0) for w in work]
+        level = 1
+        while (1 << level) < TILE:
+            mask = (((rows >> level) ^ (cols >> level)) == 1) & (rows > cols)
+            parts = [halves(x) for x in inverse]
+            links = [halves(jnp.where(mask, w["lower"], 0.0)) for w in work]
+            first = [halves(dot3(x, c)) for x, c in zip(parts, links)]
+            inverse = [x - dot3(f, p) for x, f, p in zip(inverse, first, parts)]
+            level += 1
+        for w, x in zip(work, inverse):
+            slot = w["tile"] * group + w["h"]
+            v = x_ref[
+                pl.ds(w["base"], TILE), 2 * DK + w["h"] * DV : 2 * DK + (w["h"] + 1) * DV
+            ]
+            xh, xl = halves(x * w["beta_r"])
+            pseudo[slot] = mm(xh, v) + mm(xl, v)
+            wh, wl = halves(x * w["scale_r"])
+            weights[slot] = mm(wh, w["k"]) + mm(wl, w["k"])
+            scores[slot] = w["score"]
+            keyed[slot] = jnp.where(cols == 0, w["to_end"], jnp.where(cols == 1, w["read"], 0.0))
+            ends[slot] = jnp.broadcast_to(w["from_end"], (8, TILE))
+        return carry
+
+    lax.fori_loop(0, tiles // 2, build, 0)
+
+    def advance(tile, states):
+        base = pl.multiple_of(tile * TILE, TILE)
+        q = x_ref[pl.ds(base, TILE), 0:DK]
+        k = x_ref[pl.ds(base, TILE), DK : 2 * DK]
+        following = []
+        for h in range(group):
+            slot = tile * group + h
+            state = states[h]
+            sh, sl = halves(state)
+            error = pseudo[slot] - dot3(halves(weights[slot]), (sh, sl))
+            scalars = keyed[slot]
+            eh, el = halves(error * scalars[:, 0:1])
+            grown = lax.dot_general(
+                k, eh, (((0,), (0,)), ((), ())), preferred_element_type=F32
+            ) + lax.dot_general(k, el, (((0,), (0,)), ((), ())), preferred_element_type=F32)
+            following.append(ends[slot][0:1, :] * state + grown)
+            raw = (mm(q, sh) + mm(q, sl)) * scalars[:, 1:2] + dot3(
+                halves(scores[slot]), halves(error)
+            )
+            mean = jnp.mean(raw * raw, -1, keepdims=True)
+            out_ref[pl.ds(base, TILE), h * DV : (h + 1) * DV] = (
+                raw * lax.rsqrt(mean + EPSILON) * gain_ref[...]
+            ).astype(BF)
+        return tuple(following)
+
+    lax.fori_loop(
+        0, tiles, advance, tuple(jnp.zeros((DK, DV), F32) for h in range(group))
+    )
+
+
+def mixer(lengths, rows, head_gain):
+    total = rows.shape[0]
+    group = HV // HK
+    slots = total // TILE * group
+    vmem = pl.BlockSpec(memory_space=pltpu.VMEM)
+    return pl.pallas_call(
+        mixer_kernel,
+        out_shape=jax.ShapeDtypeStruct((total, group * DV), BF),
+        in_specs=[pl.BlockSpec(memory_space=pltpu.SMEM), vmem, vmem],
+        out_specs=vmem,
+        scratch_shapes=[
+            pltpu.VMEM((slots, TILE, DV), F32),
+            pltpu.VMEM((slots, TILE, DK), F32),
+            pltpu.VMEM((slots, TILE, TILE), F32),
+            pltpu.VMEM((slots, TILE, TILE), F32),
+            pltpu.VMEM((slots, 8, TILE), F32),
+        ],
+        compiler_params=pltpu.CompilerParams(vmem_limit_bytes=40 * 1024 * 1024),
+    )(lengths, rows, head_gain.reshape(1, DV))
+
+
+def two_parts(a):
+    high = lax.reduce_precision(a, 8, 7)
+    return high.astype(BF), (a - high).astype(BF)
+
+
+def slot_table(gate_rows, capacity):
+    named = gate_rows > 0.0
+    tokens = gate_rows.shape[-1]
+    before = (
+        jnp.arange(tokens, dtype=jnp.int32)[:, None] < jnp.arange(tokens, dtype=jnp.int32)[None, :]
+    ).astype(BF)
+    rank = jnp.einsum("...t,tu->...u", named.astype(BF), before, preferred_element_type=F32)
+    slot = jnp.arange(capacity, dtype=jnp.int32).astype(F32)
+    return named[..., None, :] & (rank[..., None, :] == slot[:, None])
+
+
+def per_device(
+    queries,
+    key_in,
+    value_in,
+    gate_in,
+    residual_in,
+    log_decay,
+    beta_logit,
+    lengths,
+    head_gain,
+    out_proj,
+    post_gain,
+    expert_in,
+    expert_out,
+    routes,
+    route_gates,
+):
+    tokens = queries.shape[1]
+    n_ctx = lax.axis_size("ctx")
+    n_dp = lax.axis_size("dp")
+    local = expert_in.shape[0]
+    devices = n_ctx * n_dp
+    experts = local * devices
+    capacity = tokens * TOPK * 6 // (5 * experts)
+    group = HV // HK
+    my_dp = lax.axis_index("dp")
+    my_ctx = lax.axis_index("ctx")
+
+    ids = jnp.arange(experts, dtype=jnp.int32)[:, None]
+    gate_table = jnp.zeros((experts, tokens), F32)
+    for k in range(TOPK):
+        gate_table = gate_table + jnp.where(
+            routes[0, :, k][None, :] == ids, route_gates[0, :, k][None, :], 0.0
+        )
+    all_gates = lax.all_gather(gate_table, ("dp", "ctx"))
+
+    beta = jax.nn.sigmoid(beta_logit[0])
+    dh, dl = two_parts(log_decay[0])
+    bh, bl = two_parts(beta)
+    scal = jnp.stack([dh, dl, bh, bl]).reshape(4, n_ctx, group, tokens)
+    scal = scal.transpose(1, 3, 0, 2).reshape(n_ctx, tokens, 4 * group)
+    scal = jnp.pad(scal, ((0, 0), (0, 0), (0, SCAL - 4 * group)))
+
+    def by_head(a):
+        return a[0].reshape(tokens, n_ctx, -1).transpose(1, 0, 2)
+
+    sent = jnp.concatenate([by_head(queries), by_head(key_in), by_head(value_in), scal], -1)
+    heads = lax.all_to_all(sent, "ctx", split_axis=0, concat_axis=0, tiled=True)
+    mixed = mixer(lengths, heads.reshape(n_ctx * tokens, -1), head_gain)
+    mine = lax.all_to_all(
+        mixed.reshape(n_ctx, tokens, group * DV), "ctx", split_axis=0, concat_axis=0, tiled=True
+    )
+    unit = mine.transpose(1, 0, 2).reshape(tokens, HV * DV)
+    normed = (unit.astype(F32) * jax.nn.silu(gate_in[0].astype(F32))).astype(BF)
+    projected = jnp.dot(normed, out_proj, preferred_element_type=F32)
+    hidden_state = (residual_in[0].astype(F32) + projected).astype(BF)
+    expert_input = post_norm(hidden_state, post_gain)
+
+    column = lax.all_gather(expert_input, "dp")
+    features = lax.all_gather(column, "ctx")
+    features = features.reshape(devices, tokens, D)
+    by_dev = all_gates.reshape(n_dp, n_ctx, n_dp, n_ctx, local, tokens)
+    my_gates = lax.dynamic_index_in_dim(
+        lax.dynamic_index_in_dim(by_dev, my_dp, 2, False), my_ctx, 2, False
+    )
+    my_gates = my_gates.transpose(1, 0, 2, 3).reshape(devices, local, tokens)
+    pick = slot_table(my_gates, capacity).astype(BF).transpose(1, 0, 2, 3)
+    routed = jnp.einsum("jsct,std->jscd", pick, features, preferred_element_type=F32)
+    routed = routed.astype(BF).reshape(local, devices * capacity, D)
+    gate_up = jnp.einsum("jrd,jdf->jrf", routed, expert_in, preferred_element_type=F32)
+    hidden_units = (jax.nn.silu(gate_up[..., :FF]) * gate_up[..., FF:]).astype(BF)
+    result = jnp.einsum("jrf,jfd->jrd", hidden_units, expert_out, preferred_element_type=F32)
+    result = result.astype(BF).reshape(local, n_ctx, n_dp, capacity, D).transpose(1, 2, 0, 3, 4)
+    returned = lax.all_to_all(result, "ctx", split_axis=0, concat_axis=0, tiled=True)
+
+    plane = lax.dynamic_index_in_dim(by_dev, my_ctx, 1, False)
+    plane = lax.dynamic_index_in_dim(plane, my_dp, 1, False)
+    table = slot_table(plane, capacity)
+    weight = jnp.where(table, plane[..., None, :], 0.0).astype(BF)
+    partial = jnp.einsum("pejct,epjcd->ptd", weight, returned, preferred_element_type=F32)
+    summed = lax.all_to_all(
+        partial.astype(BF), "dp", split_axis=0, concat_axis=0, tiled=True
+    )
+    total = hidden_state.astype(F32) + jnp.sum(summed.astype(F32), 0)
+    return total.astype(BF)[None]
+
+
 def solution(mesh):
     in_specs = (
         P("dp", "ctx", None),
@@ -251,6 +544,7 @@
         P("dp", "ctx", None),
     )
     out_specs = P("dp", "ctx", None)
+    by_heads = mesh.shape["ctx"] == HK
     return jax.shard_map(
-        per_device, mesh=mesh, in_specs=in_specs, out_specs=out_specs, check_vma=False
-    )
+        per_device if by_heads else per_device_long, mesh=mesh, in_specs=in_specs, out_specs=out_specs, check_vma=False
+    )

time: 754 us -> 430 us (0.57)
  other arithmetic: 215 us -> 4.63 us
  blocking collectives: 163 us -> 85.2 us
  local copies, waits for them, and re-layouts: 86 us -> 9.76 us
  waiting for transfers between devices: 207 us -> 260 us
  matrix products: 55.3 us -> 30.5 us
  Pallas kernels: 0 us -> 20 us
    another operation x7 -> x0, other arithmetic: 195 us -> none  [the longest x2 158 us: block_terms(): jax.scipy.linalg.solve_triangular(system, right_side, lower=True, unit_di...]
    all_gather x2 -> x3, waiting for transfers between devices: 66 us -> 188 us  [the longest x1 88.7 us: per_device(): features = lax.all_gather(column, 'ctx')]
    all_to_all x1 -> x3, blocking collectives: 163 us -> 85.2 us  [the longest x1 49.6 us: per_device(): lax.all_to_all(partial.astype(BF), 'dp', split_axis=0, concat_axis=0, til...]
    all_to_all x1, waiting for transfers between devices: 140 us -> 71.3 us  [per_device(): lax.all_to_all(result, 'ctx', split_axis=0, concat_axis=0, tiled=True)]
    gather x1 -> x0, local copies, waits for them, and re-layouts: 24.2 us -> none  [per_device(): back_rows = returned.reshape(experts_all, capacity, D)[flat_ids, slot_rank]]
    dot_general x16 -> x7, matrix products: 53.3 us -> 30.5 us  [the longest x1 10.9 us: per_device(): jnp.einsum('jrd,jdf->jrf', routed, expert_in, preferred_element_type=F32)]
    pallas_call x0 -> x1, Pallas kernels: none -> 20 us  [mixer(): pl.pallas_call(mixer_kernel, out_shape=jax.ShapeDtypeStruct((total, group...]
    unnamed x45 -> x24, local copies, waits for them, and re-layouts: 17.3 us -> 3.69 us
  transfers between devices with their start and end apart: 3 -> 4, of which waited for: 3 -> 4; matrix products, arithmetic and copies ran while one was open for 6% -> 1% of each run, Pallas kernels for 0% -> 0%
where the time goes in v1:
time: 430 us; the launch traced here: 428 us
  waiting for transfers between devices  260 us (60%)
  blocking collectives  85.2 us (20%)
  matrix products  30.5 us (7%)
  Pallas kernels  20 us (5%)
  between operations  13.5 us (3%)
  local copies, waits for them, and re-layouts  9.76 us (2%)
  starting transfers between devices  5.01 us (1%)
  other arithmetic  4.63 us (1%)
    all_gather x1, waiting for transfers between devices, per_device(): features = lax.all_gather(column, 'ctx')  88.7 us
    all_to_all x1, waiting for transfers between devices, per_device(): lax.all_to_all(result, 'ctx', split_axis=0, concat_axis=0, tiled=True)  71.3 us
    all_gather x1, waiting for transfers between devices, per_device(): all_gates = lax.all_gather(gate_table, ('dp', 'ctx'))  55.2 us
    all_to_all x1, blocking collectives, per_device(): lax.all_to_all(partial.astype(BF), 'dp', split_axis=0, concat_axis=0, til...  49.6 us
    all_gather x1, waiting for transfers between devices, per_device(): column = lax.all_gather(expert_input, 'dp')  44.5 us
    all_to_all x1, blocking collectives, per_device(): heads = lax.all_to_all(sent, 'ctx', split_axis=0, concat_axis=0, tiled=True)  23.4 us
    pallas_call x1, Pallas kernels, mixer(): pl.pallas_call(mixer_kernel, out_shape=jax.ShapeDtypeStruct((total, group...  20 us
    all_to_all x1, blocking collectives, per_device(): lax.all_to_all(mixed.reshape(n_ctx, tokens, group * DV), 'ctx', split_axi...  12.2 us
  transfers between devices with their start and end apart: 4, of which 4 were waited for; matrix products, arithmetic and copies ran while one was open for 1% of the time, Pallas kernels for 0%

profile of v1, /device:TPU:0, one launch (start us, length us, event | category | flops | bytes accessed | tf_op | source)
XLA Modules:
  0.0 428.3 jit_solution(2774834871837345512)
XLA Ops:
  6.5 0.7 reduce-precision_convert_fusion.1
  7.2 0.7 reduce-precision_convert_fusion
  8.2 1.0 copy.66
  9.2 1.1 copy.67
  10.4 1.3 copy.68
  12.1 23.4 %all_to_all.20 = bf16[8,128,640]{2,1,0:T(8,128)(2,1)S(1)} all-to-all(bf16[8,128,640]{2,1,0:T(8,128)(2,1)S(1)} %fusion.10), channel_id=1, replica_groups=mesh['dp'=4,'ctx'=8] {'ctx'}, dimensions={0} | all-to-all | bytes 2621440 | tf_op jit(solution)/shard_map/all_to_all | solution.py:488
  35.5 20.0 %shard_map.145 = bf16[1024,256]{1,0:T(8,128)(2,1)S(1)} custom-call(s32[1,4]{1,0:T(1,128)S(1)} %copy-done, bf16[1024,640]{1,0:T(8,128)(2,1)S(1)} %bitcast.132, f32[1,128]{1,0:T(1,128)S(1)} %bitcast.134), custom_call_target="tpu_custom_call" | custom-call | tf_op jit(solution)/shard_map/pallas_call | solution.py:409
  55.5 12.2 %all_to_all.21 = bf16[8,128,256]{2,1,0:T(8,128)(2,1)S(1)} all-to-all(bf16[8,128,256]{2,1,0:T(8,128)(2,1)S(1)} %bitcast.133), channel_id=1, replica_groups=mesh['dp'=4,'ctx'=8] {'ctx'}, dimensions={0} | all-to-all | bytes 1048576 | tf_op jit(solution)/shard_map/all_to_all | solution.py:490
  67.9 1.6 multiply_reduce_fusion
  69.5 1.0 multiply_convert_fusion
  70.6 0.6 select_add_fusion
  71.5 44.5 %all-gather.8.cloned.1.call-done = bf16[512,2048]{1,0:T(8,128)(2,1)} async-done(((bf16[128,2048]{1,0:T(8,128)(2,1)}), bf16[512,2048]{1,0:T(8,128)(2,1)}) %all-gather.8.cloned.1.call-update) | async-done | bytes 2097168 | tf_op jit(solution)/shard_map/all_gather | solution.py:499
  116.0 55.2 %all-gather.6.cloned.1.call-done = f32[32,64,128]{2,1,0:T(8,128)} async-done(((f32[1,64,128]{2,1,0:T(8,128)}), f32[32,64,128]{2,1,0:T(8,128)}) %all-gather.6.cloned.1.call-update) | async-done | bytes 1048592 | tf_op jit(solution)/shard_map/all_gather | solution.py:475
  171.2 1.8 copy.51
  173.3 88.7 %all-gather.10.cloned.1.call-done = bf16[32,128,2048]{2,1,0:T(8,128)(2,1)} async-done(((bf16[4,128,2048]{2,1,0:T(8,128)(2,1)}), bf16[32,128,2048]{2,1,0:T(8,128)(2,1)}) %all-gather.10.cloned.1.call-update) | async-done | bytes 16777232 | tf_op jit(solution)/shard_map/all_gather | solution.py:500
  262.0 7.1 %convert_bitcast_fusion = bf16[2,32,24,2048]{3,2,0,1:T(8,128)(2,1)S(1)} fusion(bf16[32,128,2048]{2,1,0:T(8,128)(2,1)} %all-gather.10.cloned.1.call-done, f32[2,32,128]{2,0,1:T(2,128)S(1)} %copy.58, f32[24]{0:T(128)S(1)} %iota_convert_fusion, pred[2,32,128]{2,0,1:T(4,128)(4,1)S(1)} %copy.57), kind=kOutput, calls=%fused_computation.3 | convolution fusion | flops 808845312 | bytes 23109728 | tf_op jit(solution)/shard_map/jsct,std->jscd/dot_general | solution.py:508
  269.6 10.9 %fusion.41 = f32[2,768,1024]{2,1,0:T(8,128)} fusion(bf16[2,768,2048]{2,1,0:T(8,128)(2,1)S(1)} %bitcast.136, bf16[2,2048,1024]{2,1,0:T(8,128)(2,1)} %param.26), kind=kOutput, calls=%fused_computation.98 | convolution fusion | flops 6442450944 | bytes 20971520 | tf_op jit(solution)/shard_map/jrd,jdf->jrf/dot_general | solution.py:510
  280.5 6.6 %convolution_convert_fusion = bf16[2,768,2048]{2,1,0:T(8,128)(2,1)S(1)} fusion(bf16[2,512,2048]{2,1,0:T(8,128)(2,1)S(1)} %copy-done.5, f32[2,768,1024]{2,1,0:T(8,128)} %fusion.41), kind=kOutput, calls=%fused_computation.4 | convolution fusion | flops 3229089792 | bytes 16777216 | tf_op jit(solution)/shard_map/jrf,jfd->jrd/dot_general | solution.py:512
  287.1 3.2 copy.76
  290.3 4.7 %all-to-all-start.2 = ((bf16[8,4,2,24,2048]{4,3,2,1,0:T(8,128)(2,1)}), bf16[8,4,2,24,2048]{4,3,2,1,0:T(8,128)(2,1)}, u32[]{:S(2)}, u32[]{:S(2)}) async-start(bf16[8,4,2,24,2048]{4,3,2,1,0:T(8,128)(2,1)} %bitcast.135), calls=%async_computation.2 | async-start | bytes 12582912 | tf_op jit(solution)/shard_map/all_to_all | solution.py:514
  295.3 71.3 %all-to-all-done.2 = bf16[8,4,2,24,2048]{4,3,2,1,0:T(8,128)(2,1)} async-done(((bf16[8,4,2,24,2048]{4,3,2,1,0:T(8,128)(2,1)}), bf16[8,4,2,24,2048]{4,3,2,1,0:T(8,128)(2,1)}, u32[]{:S(2)}, u32[]{:S(2)}) %all-to-all-start.2) | async-done | bytes 6291488 | tf_op jit(solution)/shard_map/all_to_all | solution.py:514
  366.6 4.2 bitcast_convert_fusion
  370.8 49.6 %all_to_all.22 = bf16[4,128,2048]{2,1,0:T(8,128)(2,1)S(1)} all-to-all(bf16[4,128,2048]{2,1,0:T(8,128)(2,1)S(1)} %bitcast_convert_fusion), channel_id=1, replica_groups=mesh['dp'=4,'ctx'=8] {'dp'}, dimensions={0} | all-to-all | bytes 4194304 | tf_op jit(solution)/shard_map/all_to_all | solution.py:521
  420.8 0.9 fusion.19
  (53 shorter events, 2.6 us)
Async XLA Ops:
  6.5 109.4 %all-gather.8.cloned.1.call-start = ((), (), s32[]{:S(2)}) async-start(), calls=%async_computation.5 | async-start | bytes 2621440 | tf_op jit(solution)/shard_map/all_gather | solution.py:499
  9.2 58.6 %slice-start = ((s8[8388608]{0:T(1024)(128)(4,1)}), s8[4194304]{0:T(1024)(128)(4,1)S(1)}, s32[]{:S(2)}) async-start(s8[8388608]{0:T(1024)(128)(4,1)} %bitcast.157), calls=%async_computation.7 | async-start | bytes 8388608
  10.4 25.1 %copy-start = (s32[1,4]{1,0:T(1,128)S(1)}, s32[1,4]{1,0:T(1,128)}, u32[]{:S(2)}) copy-start(s32[1,4]{1,0:T(1,128)} %lengths_ref.1) | copy-start | bytes 52
  10.4 25.1 %copy-start.1 = (f32[128]{0:T(128)S(1)}, f32[128]{0:T(128)}, u32[]{:S(2)}) copy-start(f32[128]{0:T(128)} %param.23) | copy-start | bytes 1540
  12.1 55.8 %slice-start.1 = ((s8[8388608]{0:T(1024)(128)(4,1)}), s8[4194304]{0:T(1024)(128)(4,1)S(1)}, s32[]{:S(2)}) async-start(s8[8388608]{0:T(1024)(128)(4,1)} %bitcast.157), calls=%async_computation.8 | async-start | bytes 8388608
  12.1 55.8 %copy-start.6 = (bf16[1,128,2048]{2,1,0:T(8,128)(2,1)S(1)}, bf16[1,128,2048]{2,1,0:T(8,128)(2,1)}, u32[]{:S(2)}) copy-start(bf16[1,128,2048]{2,1,0:T(8,128)(2,1)} %param.18) | copy-start | bytes 1572868
  12.1 55.8 %copy-start.7 = (bf16[1,128,2048]{2,1,0:T(8,128)(2,1)S(1)}, bf16[1,128,2048]{2,1,0:T(8,128)(2,1)}, u32[]{:S(2)}) copy-start(bf16[1,128,2048]{2,1,0:T(8,128)(2,1)} %param.19) | copy-start | bytes 1572868
  67.9 1.6 copy-start.2
  67.9 2.6 copy-start.3
  67.9 2.6 copy-start.4
  70.5 100.7 %all-gather.6.cloned.1.call-start = ((), (), s32[]{:S(2)}) async-start(), calls=%async_computation.4 | async-start | bytes 1081344 | tf_op jit(solution)/shard_map/all_gather | solution.py:475
  71.2 190.7 %all-gather.10.cloned.1.call-start = ((), (), s32[]{:S(2)}) async-start(), calls=%async_computation.6 | async-start | bytes 18874368 | tf_op jit(solution)/shard_map/all_gather | solution.py:500
  269.6 10.9 %copy-start.5 = (bf16[2,512,2048]{2,1,0:T(8,128)(2,1)S(1)}, bf16[2,512,2048]{2,1,0:T(8,128)(2,1)}, u32[]{:S(2)}) copy-start(bf16[2,512,2048]{2,1,0:T(8,128)(2,1)} %param.27) | copy-start | bytes 12582916
  290.3 76.4 %all-to-all-start.2 = ((bf16[8,4,2,24,2048]{4,3,2,1,0:T(8,128)(2,1)}), bf16[8,4,2,24,2048]{4,3,2,1,0:T(8,128)(2,1)}, u32[]{:S(2)}, u32[]{:S(2)}) async-start(bf16[8,4,2,24,2048]{4,3,2,1,0:T(8,128)(2,1)} %bitcast.135), calls=%async_computation.2 | async-start | bytes 12582912 | tf_op jit(solution)/shard_map/all_to_all | solution.py:514
Sparse Core Ops, SparseCore 0:
  70.6 45.2 all-gather.7
  118.8 52.3 all-gather.5
  173.1 88.8 all-gather.9

commit v2 on v1

--- a/solution.py
+++ b/solution.py
@@ -1,3 +1,5 @@
+import functools
+
 import jax
 import jax.numpy as jnp
 from jax import lax
@@ -422,6 +424,200 @@
     )(lengths, rows, head_gain.reshape(1, DV))
 
 
+def moe_kernel(
+    n_dp, x_ref, hidden_ref, pick_ref, weight_ref, in_hbm, out_hbm, o_ref,
+    feat, w_in, w_out, routed, units, sent, got, part, summed,
+    load_sem, z_send, z_recv, d_send, d_recv, r_send, r_recv, p_send, p_recv,
+):
+    z = lax.axis_index("dp")
+    me = lax.axis_index("ctx")
+    tokens = x_ref.shape[0]
+    half = tokens // 2
+    rows = sent.shape[2]
+    cap = rows // 2
+    core, along_x, along_y = me % 2, (me // 2) % 2, me // 4
+
+    def beside(rel):
+        c = 1 - core if rel % 2 else core
+        x = 1 - along_x if (rel // 2) % 2 else along_x
+        y = 1 - along_y if rel // 4 else along_y
+        return (z, (y * 2 + x) * 2 + c)
+
+    def above(s):
+        return (lax.rem(z + s, n_dp), me)
+
+    def below(s):
+        return (lax.rem(z - s + n_dp, n_dp), me)
+
+    loads = [
+        pltpu.make_async_copy(in_hbm, w_in, load_sem.at[0]),
+        pltpu.make_async_copy(out_hbm, w_out, load_sem.at[1]),
+    ]
+    for copy in loads:
+        copy.start()
+    barrier = pltpu.get_barrier_semaphore()
+    peers = [above(s) for s in range(1, n_dp)] + [beside(rel) for rel in range(1, 8)]
+    for peer in peers:
+        pl.semaphore_signal(barrier, inc=1, device_id=peer, device_id_type=pl.DeviceIdType.MESH)
+    pl.semaphore_wait(barrier, len(peers))
+
+    started = []
+
+    def push(src, dst, send, recv, peer):
+        copy = pltpu.make_async_remote_copy(
+            src_ref=src, dst_ref=dst, send_sem=send, recv_sem=recv,
+            device_id=peer, device_id_type=pl.DeviceIdType.MESH,
+        )
+        copy.start()
+        started.append(copy)
+
+    def arrived(dst, send, recv, peer):
+        pltpu.make_async_remote_copy(
+            src_ref=dst, dst_ref=dst, send_sem=send, recv_sem=recv,
+            device_id=peer, device_id_type=pl.DeviceIdType.MESH,
+        ).wait_recv()
+
+    def spread(s):
+        mine = feat.at[s, 0]
+        push(mine, feat.at[s, 2], d_send.at[s, 0], d_recv.at[s, 0], beside(2))
+        push(mine, feat.at[s, 4], d_send.at[s, 1], d_recv.at[s, 1], beside(4))
+        push(mine, feat.at[s, 1], d_send.at[s, 2], d_recv.at[s, 2], beside(1))
+
+    def forward(s):
+        low, high = pl.ds(0, half), pl.ds(half, half)
+        arrived(feat.at[s, 2], d_send.at[s, 0], d_recv.at[s, 0], beside(2))
+        push(feat.at[s, 2, low], feat.at[s, 6, low], d_send.at[s, 3], d_recv.at[s, 3], beside(4))
+        push(feat.at[s, 2], feat.at[s, 3], d_send.at[s, 5], d_recv.at[s, 5], beside(1))
+        arrived(feat.at[s, 4], d_send.at[s, 1], d_recv.at[s, 1], beside(4))
+        push(feat.at[s, 4, high], feat.at[s, 6, high], d_send.at[s, 4], d_recv.at[s, 4], beside(2))
+        push(feat.at[s, 4], feat.at[s, 5], d_send.at[s, 6], d_recv.at[s, 6], beside(1))
+        arrived(feat.at[s, 6, low], d_send.at[s, 3], d_recv.at[s, 3], beside(4))
+        arrived(feat.at[s, 6, high], d_send.at[s, 4], d_recv.at[s, 4], beside(2))
+        push(feat.at[s, 6], feat.at[s, 7], d_send.at[s, 7], d_recv.at[s, 7], beside(1))
+
+    def complete(s):
+        for rel, kind in ((1, 2), (3, 5), (5, 6), (7, 7)):
+            arrived(feat.at[s, rel], d_send.at[s, kind], d_recv.at[s, kind], beside(1))
+
+    def experts(s):
+        wide = 512
+
+        def choose(n, carry):
+            at = pl.ds(pl.multiple_of(n * wide, wide), wide)
+            found = [mm(pick_ref[s, rel], feat[s, rel, :, at]) for rel in range(8)]
+            for j in range(2):
+                routed[j, :, at] = jnp.concatenate(
+                    [f[j * cap : (j + 1) * cap] for f in found], 0
+                ).astype(BF)
+            return carry
+
+        lax.fori_loop(0, D // wide, choose, 0)
+        if s == 0:
+            for copy in loads:
+                copy.wait()
+        step = 256
+        for j in range(2):
+
+            def lift(n, carry):
+                lo = pl.multiple_of(n * step, step)
+                g = mm(routed[j], w_in[j, :, pl.ds(lo, step)])
+                u = mm(routed[j], w_in[j, :, pl.ds(lo + FF, step)])
+                units[j, :, pl.ds(lo, step)] = (g / (1.0 + jnp.exp(-g)) * u).astype(BF)
+                return carry
+
+            lax.fori_loop(0, FF // step, lift, 0)
+
+        def lower(n, carry):
+            at = pl.ds(pl.multiple_of(n * wide, wide), wide)
+            y = [mm(units[j], w_out[j, :, at]) for j in range(2)]
+            for rel in range(8):
+                block = jnp.concatenate([v[rel * cap : (rel + 1) * cap] for v in y], 0).astype(BF)
+                if rel == 0:
+                    got[s, 0, :, at] = block
+                else:
+                    sent[s, rel, :, at] = block
+            return carry
+
+        lax.fori_loop(0, D // wide, lower, 0)
+        for rel in (6, 7, 2, 4, 3, 5, 1):
+            push(sent.at[s, rel], got.at[s, rel], r_send.at[s, rel], r_recv.at[s, rel], beside(rel))
+
+    def combine(s):
+        for rel in range(1, 8):
+            arrived(got.at[s, rel], r_send.at[s, rel], r_recv.at[s, rel], beside(rel))
+        wide = 512
+
+        def mix(n, carry):
+            at = pl.ds(pl.multiple_of(n * wide, wide), wide)
+            part[s, :, at] = mm(
+                weight_ref[s], got[s, :, :, at].reshape(8 * rows, wide)
+            ).astype(BF)
+            return carry
+
+        lax.fori_loop(0, D // wide, mix, 0)
+        if s:
+            push(part.at[s], summed.at[s], p_send.at[s], p_recv.at[s], below(s))
+
+    feat[0, 0] = x_ref[...]
+    spread(0)
+    for s in range(1, n_dp):
+        push(feat.at[0, 0], feat.at[s, 0], z_send.at[s], z_recv.at[s], above(s))
+    for s in range(n_dp):
+        if s + 1 < n_dp:
+            arrived(feat.at[s + 1, 0], z_send.at[s + 1], z_recv.at[s + 1], below(s + 1))
+            spread(s + 1)
+        forward(s)
+        complete(s)
+        experts(s)
+        if s:
+            combine(s - 1)
+    combine(n_dp - 1)
+    total = hidden_ref[...].astype(F32) + part[0].astype(F32)
+    for s in range(1, n_dp):
+        arrived(summed.at[s], p_send.at[s], p_recv.at[s], above(s))
+        total = total + summed[s].astype(F32)
+    o_ref[...] = total.astype(BF)
+    for copy in started:
+        copy.wait_send()
+
+
+def moe(n_dp, expert_input, hidden_state, pick, weight, expert_in, expert_out):
+    tokens = expert_input.shape[0]
+    rows = pick.shape[2]
+    vmem = pl.BlockSpec(memory_space=pltpu.VMEM)
+    hbm = pl.BlockSpec(memory_space=pl.ANY)
+    dma = pltpu.SemaphoreType.DMA
+    return pl.pallas_call(
+        functools.partial(moe_kernel, n_dp),
+        out_shape=jax.ShapeDtypeStruct((tokens, D), BF),
+        in_specs=[vmem, vmem, vmem, vmem, hbm, hbm],
+        out_specs=vmem,
+        scratch_shapes=[
+            pltpu.VMEM((n_dp, 8, tokens, D), BF),
+            pltpu.VMEM(expert_in.shape, BF),
+            pltpu.VMEM(expert_out.shape, BF),
+            pltpu.VMEM((2, 4 * rows, D), BF),
+            pltpu.VMEM((2, 4 * rows, FF), BF),
+            pltpu.VMEM((n_dp, 8, rows, D), BF),
+            pltpu.VMEM((n_dp, 8, rows, D), BF),
+            pltpu.VMEM((n_dp, tokens, D), BF),
+            pltpu.VMEM((n_dp, tokens, D), BF),
+            dma((2,)),
+            dma((n_dp,)),
+            dma((n_dp,)),
+            dma((n_dp, 8)),
+            dma((n_dp, 8)),
+            dma((n_dp, 8)),
+            dma((n_dp, 8)),
+            dma((n_dp,)),
+            dma((n_dp,)),
+        ],
+        compiler_params=pltpu.CompilerParams(
+            collective_id=0, has_side_effects=True, vmem_limit_bytes=60 * 1024 * 1024
+        ),
+    )(expert_input, hidden_state, pick, weight, expert_in, expert_out)
+
+
 def two_parts(a):
     high = lax.reduce_precision(a, 8, 7)
     return high.astype(BF), (a - high).astype(BF)
@@ -472,20 +668,26 @@
         gate_table = gate_table + jnp.where(
             routes[0, :, k][None, :] == ids, route_gates[0, :, k][None, :], 0.0
         )
-    all_gates = lax.all_gather(gate_table, ("dp", "ctx"))
+    gate_table = gate_table.astype(BF)
+    column_gates = lax.all_gather(gate_table, "dp")
+    gate_cols = gate_table.reshape(n_dp, n_ctx, local, tokens).transpose(1, 3, 0, 2)
+    gate_cols = gate_cols.reshape(n_ctx, tokens, n_dp * local)
 
     beta = jax.nn.sigmoid(beta_logit[0])
     dh, dl = two_parts(log_decay[0])
     bh, bl = two_parts(beta)
     scal = jnp.stack([dh, dl, bh, bl]).reshape(4, n_ctx, group, tokens)
     scal = scal.transpose(1, 3, 0, 2).reshape(n_ctx, tokens, 4 * group)
-    scal = jnp.pad(scal, ((0, 0), (0, 0), (0, SCAL - 4 * group)))
+    scal = jnp.concatenate([scal, gate_cols], -1)
+    scal = jnp.pad(scal, ((0, 0), (0, 0), (0, SCAL - scal.shape[-1])))
 
     def by_head(a):
         return a[0].reshape(tokens, n_ctx, -1).transpose(1, 0, 2)
 
     sent = jnp.concatenate([by_head(queries), by_head(key_in), by_head(value_in), scal], -1)
     heads = lax.all_to_all(sent, "ctx", split_axis=0, concat_axis=0, tiled=True)
+    gates_at = 2 * DK + group * DV + 4 * group
+    plane_gates = lax.all_gather(heads[:, :, gates_at : gates_at + n_dp * local], "dp")
     mixed = mixer(lengths, heads.reshape(n_ctx * tokens, -1), head_gain)
     mine = lax.all_to_all(
         mixed.reshape(n_ctx, tokens, group * DV), "ctx", split_axis=0, concat_axis=0, tiled=True
@@ -496,33 +698,18 @@
     hidden_state = (residual_in[0].astype(F32) + projected).astype(BF)
     expert_input = post_norm(hidden_state, post_gain)
 
-    column = lax.all_gather(expert_input, "dp")
-    features = lax.all_gather(column, "ctx")
-    features = features.reshape(devices, tokens, D)
-    by_dev = all_gates.reshape(n_dp, n_ctx, n_dp, n_ctx, local, tokens)
-    my_gates = lax.dynamic_index_in_dim(
-        lax.dynamic_index_in_dim(by_dev, my_dp, 2, False), my_ctx, 2, False
-    )
-    my_gates = my_gates.transpose(1, 0, 2, 3).reshape(devices, local, tokens)
-    pick = slot_table(my_gates, capacity).astype(BF).transpose(1, 0, 2, 3)
-    routed = jnp.einsum("jsct,std->jscd", pick, features, preferred_element_type=F32)
-    routed = routed.astype(BF).reshape(local, devices * capacity, D)
-    gate_up = jnp.einsum("jrd,jdf->jrf", routed, expert_in, preferred_element_type=F32)
-    hidden_units = (jax.nn.silu(gate_up[..., :FF]) * gate_up[..., FF:]).astype(BF)
-    result = jnp.einsum("jrf,jfd->jrd", hidden_units, expert_out, preferred_element_type=F32)
-    result = result.astype(BF).reshape(local, n_ctx, n_dp, capacity, D).transpose(1, 2, 0, 3, 4)
-    returned = lax.all_to_all(result, "ctx", split_axis=0, concat_axis=0, tiled=True)
-
-    plane = lax.dynamic_index_in_dim(by_dev, my_ctx, 1, False)
-    plane = lax.dynamic_index_in_dim(plane, my_dp, 1, False)
-    table = slot_table(plane, capacity)
-    weight = jnp.where(table, plane[..., None, :], 0.0).astype(BF)
-    partial = jnp.einsum("pejct,epjcd->ptd", weight, returned, preferred_element_type=F32)
-    summed = lax.all_to_all(
-        partial.astype(BF), "dp", split_axis=0, concat_axis=0, tiled=True
-    )
-    total = hidden_state.astype(F32) + jnp.sum(summed.astype(F32), 0)
-    return total.astype(BF)[None]
+    packs = (my_dp - jnp.arange(n_dp)) % n_dp
+    places = my_ctx ^ jnp.arange(n_ctx)
+    my_gates = plane_gates.reshape(n_dp, n_ctx, tokens, n_dp, local)
+    my_gates = lax.dynamic_index_in_dim(my_gates, my_dp, 3, False).transpose(0, 1, 3, 2)
+    my_gates = my_gates[packs][:, places]
+    pick = slot_table(my_gates, capacity).astype(BF)
+    pick = pick.reshape(n_dp, n_ctx, local * capacity, tokens)
+    plane = column_gates.reshape(n_dp, n_dp, n_ctx, local, tokens)
+    plane = lax.dynamic_index_in_dim(plane, my_dp, 1, False)[packs][:, places]
+    weight = jnp.where(slot_table(plane, capacity), plane[..., None, :], 0)
+    weight = weight.reshape(n_dp, n_ctx * local * capacity, tokens).transpose(0, 2, 1)
+    return moe(n_dp, expert_input, hidden_state, pick, weight, expert_in, expert_out)[None]
 
 
 def solution(mesh):

time: 430 us -> 288 us (0.67)
  waiting for transfers between devices: 260 us -> 1.14 us
  Pallas kernels: 20 us -> 225 us
  blocking collectives: 85.2 us -> 26.9 us
  matrix products: 30.5 us -> 5.25 us
  between operations: 13.5 us -> 0.38 us
    pallas_call x0 -> x1, Pallas kernels: none -> 204 us  [moe(): pl.pallas_call(functools.partial(moe_kernel, n_dp), out_shape=jax.ShapeDt...]
    all_gather x3 -> x0, waiting for transfers between devices: 188 us -> none  [the longest x1 88.7 us: per_device(): features = lax.all_gather(column, 'ctx')]
    all_to_all x3 -> x0, blocking collectives: 85.2 us -> none  [the longest x1 49.6 us: per_device(): lax.all_to_all(partial.astype(BF), 'dp', split_axis=0, concat_axis=0, til...]
    all_to_all x1 -> x2, waiting for transfers between devices: 71.3 us -> 1.14 us  [the longest x1 1.13 us: per_device(): heads = lax.all_to_all(sent, 'ctx', split_axis=0, concat_axis=0, tiled=True)]
    dot_general x4 -> x0, matrix products: 28.7 us -> none  [the longest x1 10.9 us: per_device(): jnp.einsum('jrd,jdf->jrf', routed, expert_in, preferred_element_type=F32)]
    all_gather x0 -> x2, blocking collectives: none -> 26.9 us  [the longest x1 13.6 us: per_device(): lax.all_gather(heads[:, :, gates_at:gates_at + n_dp * local], 'dp')]
    all_to_all x1 -> x2, starting transfers between devices: 4.75 us -> 8.8 us  [the longest x1 5.17 us: per_device(): heads = lax.all_to_all(sent, 'ctx', split_axis=0, concat_axis=0, tiled=True)]
  transfers between devices with their start and end apart: 4 -> 2, of which waited for: 4 -> 1; matrix products, arithmetic and copies ran while one was open for 1% -> 2% of each run, Pallas kernels for 0% -> 0%
where the time goes in v2:
time: 288 us; the launch traced here: 285 us
  Pallas kernels  225 us (78%)
  blocking collectives  26.9 us (9%)
  local copies, waits for them, and re-layouts  11.7 us (4%)
  starting transfers between devices  8.8 us (3%)
  other arithmetic  5.88 us (2%)
  matrix products  5.25 us (2%)
    pallas_call x1, Pallas kernels, moe(): pl.pallas_call(functools.partial(moe_kernel, n_dp), out_shape=jax.ShapeDt...  204 us
    pallas_call x1, Pallas kernels, mixer(): pl.pallas_call(mixer_kernel, out_shape=jax.ShapeDtypeStruct((total, group...  20.8 us
    all_gather x1, blocking collectives, per_device(): lax.all_gather(heads[:, :, gates_at:gates_at + n_dp * local], 'dp')  13.6 us
    all_gather x1, blocking collectives, per_device(): column_gates = lax.all_gather(gate_table, 'dp')  13.3 us
  transfers between devices with their start and end apart: 2, of which 1 were waited for; matrix products, arithmetic and copies ran while one was open for 2% of the time, Pallas kernels for 0%

profile of v2, /device:TPU:0, one launch (start us, length us, event | category | flops | bytes accessed | tf_op | source)
XLA Modules:
  0.0 284.6 jit_solution(7744159043335421338)
XLA Ops:
  0.0 0.8 slice_bitcast_fusion.19
  0.8 0.8 slice_bitcast_fusion.18
  1.8 0.7 reduce-precision_convert_fusion
  2.5 0.7 reduce-precision_convert_fusion.1
  3.2 1.3 copy.84
  4.6 1.1 copy.82
  5.7 1.1 copy.83
  7.0 1.2 pad_maximum_fusion
  8.2 5.2 %all-to-all-start = ((bf16[8,128,640]{1,2,0:T(8,128)(2,1)}), bf16[8,128,640]{1,2,0:T(8,128)(2,1)S(1)}, u32[]{:S(2)}, u32[]{:S(2)}) async-start(bf16[8,128,640]{1,2,0:T(8,128)(2,1)} %pad_maximum_fusion), calls=%async_computation | async-start | bytes 2621440 | tf_op jit(solution)/shard_map/all_to_all | solution.py:688
  13.5 13.3 %all_gather.12 = bf16[4,64,128]{2,1,0:T(8,128)(2,1)S(1)} all-gather(bf16[1,64,128]{2,1,0:T(8,128)(2,1)S(1)} %add_convert_fusion), channel_id=1, replica_groups=mesh['dp'=4,'ctx'=8] {'dp'}, dimensions={0}, use_global_device_ids=true | all-gather | bytes 81920 | tf_op jit(solution)/shard_map/all_gather | solution.py:672
  26.9 0.6 gather_fusion.2
  27.5 0.6 gather_fusion.3
  29.5 0.9 fusion.16.weight_ref
  30.4 1.1 all-to-all-done
  31.6 0.7 copy.87
  32.3 20.8 %shard_map.145 = bf16[1024,256]{1,0:T(8,128)(2,1)} custom-call(s32[1,4]{1,0:T(1,128)S(1)} %copy-done, bf16[1024,640]{1,0:T(8,128)(2,1)S(1)} %bitcast.114, f32[1,128]{1,0:T(1,128)S(1)} %bitcast.115), custom_call_target="tpu_custom_call" | custom-call | tf_op jit(solution)/shard_map/pallas_call | solution.py:411
  53.1 3.6 %all-to-all-start.1 = ((bf16[8,128,256]{2,1,0:T(8,128)(2,1)}), bf16[8,128,256]{2,1,0:T(8,128)(2,1)S(1)}, u32[]{:S(2)}, u32[]{:S(2)}) async-start(bf16[8,128,256]{2,1,0:T(8,128)(2,1)} %bitcast.35), calls=%async_computation.1 | async-start | bytes 1048576 | tf_op jit(solution)/shard_map/all_to_all | solution.py:692
  56.7 13.6 %all-gather = bf16[32,128,8]{1,2,0:T(8,128)(2,1)S(1)} all-gather(bf16[8,128,8]{1,2,0:T(8,128)(2,1)S(1)} %slice.92), channel_id=2, replica_groups=mesh['dp'=4,'ctx'=8] {'dp'}, dimensions={0}, use_global_device_ids=true | all-gather | bytes 81920 | tf_op jit(solution)/shard_map/all_gather | solution.py:690
  70.9 0.6 gather_fusion.1
  71.7 1.0 fusion.10.pick_ref
  72.9 5.0 %fusion.1 = (f32[128]{0:T(128)S(1)}, bf16[128,2048]{1,0:T(8,128)(2,1)S(1)}) fusion(bf16[2048,2048]{1,0:T(8,128)(2,1)} %param.24, f32[128,2048]{1,0:T(8,128)S(1)} %bitcast.122, bf16[1,128,2048]{2,1,0:T(8,128)(2,1)S(1)} %copy-done.4, bf16[1,128,2048]{2,1,0:T(8,128)(2,1)S(1)} %copy-done.5), kind=kOutput, calls=%fused_computation.11 | convolution fusion | flops 1077149568 | bytes 11010560 | tf_op jit(solution)/shard_map/dot_general | solution.py:697
  77.9 1.0 fusion.3.x_ref
  78.9 203.8 %shard_map.146 = bf16[128,2048]{1,0:T(8,128)(2,1)} custom-call(bf16[128,2048]{1,0:T(8,128)(2,1)} %fusion.3.x_ref, bf16[128,2048]{1,0:T(8,128)(2,1)} %copy-done.2, bf16[4,8,48,128]{3,2,1,0:T(8,128)(2,1)} %fusion.10.pick_ref, bf16[4,128,384]{2,1,0:T(8,128)(2,1)} %fusion.16.weight_ref, bf16[2,2048,1024]{2,1,0:T(8,128)(2,1)} %in_hbm.1, bf16[2,512,2048]{2,1,0:T(8,128)(2,1)} %out_hbm.1), custom_call_target="tpu_custom_call" | custom-call | tf_op jit(solution)/shard_map/pallas_call | solution.py:590
  282.7 1.9 copy.116
  (59 shorter events, 2.9 us)
Async XLA Ops:
  8.2 23.4 %all-to-all-start = ((bf16[8,128,640]{1,2,0:T(8,128)(2,1)}), bf16[8,128,640]{1,2,0:T(8,128)(2,1)S(1)}, u32[]{:S(2)}, u32[]{:S(2)}) async-start(bf16[8,128,640]{1,2,0:T(8,128)(2,1)} %pad_maximum_fusion), calls=%async_computation | async-start | bytes 2621440 | tf_op jit(solution)/shard_map/all_to_all | solution.py:688
  29.0 3.3 %copy-start = (s32[1,4]{1,0:T(1,128)S(1)}, s32[1,4]{1,0:T(1,128)}, u32[]{:S(2)}) copy-start(s32[1,4]{1,0:T(1,128)} %lengths_ref.1) | copy-start | bytes 52
  29.0 3.3 %copy-start.1 = (f32[128]{0:T(128)S(1)}, f32[128]{0:T(128)}, u32[]{:S(2)}) copy-start(f32[128]{0:T(128)} %param.23) | copy-start | bytes 1540
  53.1 19.8 %copy-start.4 = (bf16[1,128,2048]{2,1,0:T(8,128)(2,1)S(1)}, bf16[1,128,2048]{2,1,0:T(8,128)(2,1)}, u32[]{:S(2)}) copy-start(bf16[1,128,2048]{2,1,0:T(8,128)(2,1)} %param.18) | copy-start | bytes 1572868
  53.1 19.8 %copy-start.5 = (bf16[1,128,2048]{2,1,0:T(8,128)(2,1)S(1)}, bf16[1,128,2048]{2,1,0:T(8,128)(2,1)}, u32[]{:S(2)}) copy-start(bf16[1,128,2048]{2,1,0:T(8,128)(2,1)} %param.19) | copy-start | bytes 1572868
  53.1 19.6 %all-to-all-start.1 = ((bf16[8,128,256]{2,1,0:T(8,128)(2,1)}), bf16[8,128,256]{2,1,0:T(8,128)(2,1)S(1)}, u32[]{:S(2)}, u32[]{:S(2)}) async-start(bf16[8,128,256]{2,1,0:T(8,128)(2,1)} %bitcast.35), calls=%async_computation.1 | async-start | bytes 1048576 | tf_op jit(solution)/shard_map/all_to_all | solution.py:692
  72.9 5.0 %copy-start.3 = (f32[2048]{0:T(1024)S(1)}, f32[2048]{0:T(1024)}, u32[]{:S(2)}) copy-start(f32[2048]{0:T(1024)} %param.25) | copy-start | bytes 24580
  77.8 1.0 copy-start.2

commit v3 on v2

--- a/solution.py
+++ b/solution.py
@@ -443,11 +443,11 @@
         y = 1 - along_y if rel // 4 else along_y
         return (z, (y * 2 + x) * 2 + c)
 
-    def above(s):
-        return (lax.rem(z + s, n_dp), me)
-
-    def below(s):
-        return (lax.rem(z - s + n_dp, n_dp), me)
+    far = z // 2
+    inner = z + far * (3 - 2 * z)
+    order = [d + far * (3 - 2 * d) for d in (inner, 1 - inner, 2, 3)]
+    inward = (z + 1 - 2 * far, me)
+    outward = (lax.rem(z + n_dp - 1 + 2 * far, n_dp), me)
 
     loads = [
         pltpu.make_async_copy(in_hbm, w_in, load_sem.at[0]),
@@ -456,7 +456,7 @@
     for copy in loads:
         copy.start()
     barrier = pltpu.get_barrier_semaphore()
-    peers = [above(s) for s in range(1, n_dp)] + [beside(rel) for rel in range(1, 8)]
+    peers = [(lax.rem(z + s, n_dp), me) for s in range(1, n_dp)] + [beside(rel) for rel in range(1, 8)]
     for peer in peers:
         pl.semaphore_signal(barrier, inc=1, device_id=peer, device_id_type=pl.DeviceIdType.MESH)
     pl.semaphore_wait(barrier, len(peers))
@@ -499,7 +499,7 @@
         for rel, kind in ((1, 2), (3, 5), (5, 6), (7, 7)):
             arrived(feat.at[s, rel], d_send.at[s, kind], d_recv.at[s, kind], beside(1))
 
-    def experts(s):
+    def experts(s, load):
         wide = 512
 
         def choose(n, carry):
@@ -512,7 +512,7 @@
             return carry
 
         lax.fori_loop(0, D // wide, choose, 0)
-        if s == 0:
+        if load:
             for copy in loads:
                 copy.wait()
         step = 256
@@ -542,7 +542,7 @@
         for rel in (6, 7, 2, 4, 3, 5, 1):
             push(sent.at[s, rel], got.at[s, rel], r_send.at[s, rel], r_recv.at[s, rel], beside(rel))
 
-    def combine(s):
+    def combine(s, remote):
         for rel in range(1, 8):
             arrived(got.at[s, rel], r_send.at[s, rel], r_recv.at[s, rel], beside(rel))
         wide = 512
@@ -555,28 +555,67 @@
             return carry
 
         lax.fori_loop(0, D // wide, mix, 0)
-        if s:
-            push(part.at[s], summed.at[s], p_send.at[s], p_recv.at[s], below(s))
-
-    feat[0, 0] = x_ref[...]
-    spread(0)
-    for s in range(1, n_dp):
-        push(feat.at[0, 0], feat.at[s, 0], z_send.at[s], z_recv.at[s], above(s))
-    for s in range(n_dp):
-        if s + 1 < n_dp:
-            arrived(feat.at[s + 1, 0], z_send.at[s + 1], z_recv.at[s + 1], below(s + 1))
-            spread(s + 1)
-        forward(s)
-        complete(s)
-        experts(s)
-        if s:
-            combine(s - 1)
-    combine(n_dp - 1)
-    total = hidden_ref[...].astype(F32) + part[0].astype(F32)
-    for s in range(1, n_dp):
-        arrived(summed.at[s], p_send.at[s], p_recv.at[s], above(s))
-        total = total + summed[s].astype(F32)
+        if remote:
+            push(part.at[s], summed.at[z], p_send.at[s], p_recv.at[z], (s, me))
+
+    def along(place, slot, peer):
+        d = order[place]
+        return pltpu.make_async_remote_copy(
+            src_ref=feat.at[d, 0], dst_ref=feat.at[d, 0], send_sem=z_send.at[slot],
+            recv_sem=z_recv.at[d], device_id=peer, device_id_type=pl.DeviceIdType.MESH,
+        )
+
+    def take(place):
+        d = order[place]
+        along(place, 0, inward).wait_recv()
+
+        @pl.when(inner == 1)
+        def pass_on():
+            along(place, place + 1, inward if place == 1 else outward).start()
+
+        spread(d)
+
+    own, first, second, third = order
+    feat[own, 0] = x_ref[...]
+    along(0, 0, inward).start()
+
+    @pl.when(inner == 1)
+    def both_ways():
+        along(0, 1, outward).start()
+
+    spread(own)
+    take(1)
+    forward(own)
+    take(2)
+    forward(first)
+    take(3)
+    complete(first)
+    experts(first, True)
+    forward(second)
+    complete(second)
+    experts(second, False)
+    forward(third)
+    complete(third)
+    experts(third, False)
+    combine(first, True)
+    complete(own)
+    experts(own, False)
+    combine(second, True)
+    combine(third, True)
+    combine(own, False)
+    total = hidden_ref[...].astype(F32) + part[own].astype(F32)
+    for d in (first, second, third):
+        arrived(summed.at[d], p_send.at[d], p_recv.at[d], (d, me))
+        total = total + summed[d].astype(F32)
     o_ref[...] = total.astype(BF)
+    along(0, 0, inward).wait_send()
+
+    @pl.when(inner == 1)
+    def passed():
+        along(0, 1, outward).wait_send()
+        for place in range(1, n_dp):
+            along(place, place + 1, inward if place == 1 else outward).wait_send()
+
     for copy in started:
         copy.wait_send()
 
@@ -603,7 +642,7 @@
             pltpu.VMEM((n_dp, tokens, D), BF),
             pltpu.VMEM((n_dp, tokens, D), BF),
             dma((2,)),
-            dma((n_dp,)),
+            dma((n_dp + 1,)),
             dma((n_dp,)),
             dma((n_dp, 8)),
             dma((n_dp, 8)),
@@ -698,15 +737,14 @@
     hidden_state = (residual_in[0].astype(F32) + projected).astype(BF)
     expert_input = post_norm(hidden_state, post_gain)
 
-    packs = (my_dp - jnp.arange(n_dp)) % n_dp
     places = my_ctx ^ jnp.arange(n_ctx)
     my_gates = plane_gates.reshape(n_dp, n_ctx, tokens, n_dp, local)
     my_gates = lax.dynamic_index_in_dim(my_gates, my_dp, 3, False).transpose(0, 1, 3, 2)
-    my_gates = my_gates[packs][:, places]
+    my_gates = my_gates[:, places]
     pick = slot_table(my_gates, capacity).astype(BF)
     pick = pick.reshape(n_dp, n_ctx, local * capacity, tokens)
     plane = column_gates.reshape(n_dp, n_dp, n_ctx, local, tokens)
-    plane = lax.dynamic_index_in_dim(plane, my_dp, 1, False)[packs][:, places]
+    plane = lax.dynamic_index_in_dim(plane, my_dp, 1, False)[:, places]
     weight = jnp.where(slot_table(plane, capacity), plane[..., None, :], 0)
     weight = weight.reshape(n_dp, n_ctx * local * capacity, tokens).transpose(0, 2, 1)
     return moe(n_dp, expert_input, hidden_state, pick, weight, expert_in, expert_out)[None]
@@ -731,7 +769,7 @@
         P("dp", "ctx", None),
     )
     out_specs = P("dp", "ctx", None)
-    by_heads = mesh.shape["ctx"] == HK
+    by_heads = mesh.shape["ctx"] == HK and mesh.shape["dp"] == 4
     return jax.shard_map(
         per_device if by_heads else per_device_long, mesh=mesh, in_specs=in_specs, out_specs=out_specs, check_vma=False
     )

time: 288 us -> 264 us (0.917)
  Pallas kernels: 225 us -> 203 us
    pallas_call x1, Pallas kernels: 204 us -> 182 us  [moe(): pl.pallas_call(functools.partial(moe_kernel, n_dp), out_shape=jax.ShapeDt...]
where the time goes in v3:
time: 264 us; the launch traced here: 262 us
  Pallas kernels  203 us (77%)
  blocking collectives  26.9 us (10%)
  local copies, waits for them, and re-layouts  10.5 us (4%)
  starting transfers between devices  8.8 us (3%)
  other arithmetic  5.85 us (2%)
  matrix products  5.21 us (2%)
    pallas_call x1, Pallas kernels, moe(): pl.pallas_call(functools.partial(moe_kernel, n_dp), out_shape=jax.ShapeDt...  182 us
    pallas_call x1, Pallas kernels, mixer(): pl.pallas_call(mixer_kernel, out_shape=jax.ShapeDtypeStruct((total, group...  20.7 us
    all_gather x1, blocking collectives, per_device(): lax.all_gather(heads[:, :, gates_at:gates_at + n_dp * local], 'dp')  13.6 us
    all_gather x1, blocking collectives, per_device(): column_gates = lax.all_gather(gate_table, 'dp')  13.3 us
    unnamed x17, local copies, waits for them, and re-layouts  5.47 us
  transfers between devices with their start and end apart: 2, of which 1 were waited for; matrix products, arithmetic and copies ran while one was open for 2% of the time, Pallas kernels for 0%

profile of v3, /device:TPU:0, one launch (start us, length us, event | category | flops | bytes accessed | tf_op | source)
XLA Modules:
  0.0 262.3 jit_solution(18444983747735942852)
XLA Ops:
  0.0 0.8 slice_bitcast_fusion.19
  0.8 0.8 slice_bitcast_fusion.18
  1.8 0.7 reduce-precision_convert_fusion
  2.5 0.7 reduce-precision_convert_fusion.1
  3.2 1.3 copy.62
  4.6 1.1 copy.60
  5.7 1.1 copy.61
  7.0 1.2 pad_maximum_fusion
  8.2 5.2 %all-to-all-start = ((bf16[8,128,640]{1,2,0:T(8,128)(2,1)}), bf16[8,128,640]{1,2,0:T(8,128)(2,1)S(1)}, u32[]{:S(2)}, u32[]{:S(2)}) async-start(bf16[8,128,640]{1,2,0:T(8,128)(2,1)} %pad_maximum_fusion), calls=%async_computation | async-start | bytes 2621440 | tf_op jit(solution)/shard_map/all_to_all | solution.py:727
  13.5 13.3 %all_gather.12 = bf16[4,64,128]{2,1,0:T(8,128)(2,1)S(1)} all-gather(bf16[1,64,128]{2,1,0:T(8,128)(2,1)S(1)} %add_convert_fusion), channel_id=1, replica_groups=mesh['dp'=4,'ctx'=8] {'dp'}, dimensions={0}, use_global_device_ids=true | all-gather | bytes 81920 | tf_op jit(solution)/shard_map/all_gather | solution.py:711
  26.9 0.6 gather_fusion.1
  28.4 0.3 copy.78
  28.9 0.9 fusion.16.weight_ref
  29.8 1.7 all-to-all-done
  31.6 0.7 copy.65
  32.3 20.7 %shard_map.145 = bf16[1024,256]{1,0:T(8,128)(2,1)} custom-call(s32[1,4]{1,0:T(1,128)S(1)} %copy-done, bf16[1024,640]{1,0:T(8,128)(2,1)S(1)} %bitcast.113, f32[1,128]{1,0:T(1,128)S(1)} %bitcast.114), custom_call_target="tpu_custom_call" | custom-call | tf_op jit(solution)/shard_map/pallas_call | solution.py:411
  53.1 3.6 %all-to-all-start.1 = ((bf16[8,128,256]{2,1,0:T(8,128)(2,1)}), bf16[8,128,256]{2,1,0:T(8,128)(2,1)S(1)}, u32[]{:S(2)}, u32[]{:S(2)}) async-start(bf16[8,128,256]{2,1,0:T(8,128)(2,1)} %bitcast.35), calls=%async_computation.1 | async-start | bytes 1048576 | tf_op jit(solution)/shard_map/all_to_all | solution.py:731
  56.7 13.6 %all-gather = bf16[32,128,8]{1,2,0:T(8,128)(2,1)S(1)} all-gather(bf16[8,128,8]{1,2,0:T(8,128)(2,1)S(1)} %slice.88), channel_id=2, replica_groups=mesh['dp'=4,'ctx'=8] {'dp'}, dimensions={0}, use_global_device_ids=true | all-gather | bytes 81920 | tf_op jit(solution)/shard_map/all_gather | solution.py:729
  70.3 0.6 gather_fusion
  71.1 1.0 fusion.10.pick_ref
  72.3 4.9 %fusion.1 = (f32[128]{0:T(128)S(1)}, bf16[128,2048]{1,0:T(8,128)(2,1)S(1)}) fusion(bf16[2048,2048]{1,0:T(8,128)(2,1)} %param.24, f32[128,2048]{1,0:T(8,128)S(1)} %bitcast.121, bf16[1,128,2048]{2,1,0:T(8,128)(2,1)S(1)} %copy-done.4, bf16[1,128,2048]{2,1,0:T(8,128)(2,1)S(1)} %copy-done.5), kind=kOutput, calls=%fused_computation.9 | convolution fusion | flops 1077149568 | bytes 11010560 | tf_op jit(solution)/shard_map/dot_general | solution.py:736
  77.2 1.0 fusion.3.x_ref
  78.2 182.1 %shard_map.146 = bf16[128,2048]{1,0:T(8,128)(2,1)} custom-call(bf16[128,2048]{1,0:T(8,128)(2,1)} %fusion.3.x_ref, bf16[128,2048]{1,0:T(8,128)(2,1)} %copy-done.2, bf16[4,8,48,128]{3,2,1,0:T(8,128)(2,1)} %fusion.10.pick_ref, bf16[4,128,384]{2,1,0:T(8,128)(2,1)} %fusion.16.weight_ref, bf16[2,2048,1024]{2,1,0:T(8,128)(2,1)} %in_hbm.1, bf16[2,512,2048]{2,1,0:T(8,128)(2,1)} %out_hbm.1), custom_call_target="tpu_custom_call" | custom-call | tf_op jit(solution)/shard_map/pallas_call | solution.py:629
  260.4 1.9 copy.97
  (54 shorter events, 2.0 us)
Async XLA Ops:
  8.2 23.4 %all-to-all-start = ((bf16[8,128,640]{1,2,0:T(8,128)(2,1)}), bf16[8,128,640]{1,2,0:T(8,128)(2,1)S(1)}, u32[]{:S(2)}, u32[]{:S(2)}) async-start(bf16[8,128,640]{1,2,0:T(8,128)(2,1)} %pad_maximum_fusion), calls=%async_computation | async-start | bytes 2621440 | tf_op jit(solution)/shard_map/all_to_all | solution.py:727
  28.3 3.9 %copy-start = (s32[1,4]{1,0:T(1,128)S(1)}, s32[1,4]{1,0:T(1,128)}, u32[]{:S(2)}) copy-start(s32[1,4]{1,0:T(1,128)} %lengths_ref.1) | copy-start | bytes 52
  28.3 3.9 %copy-start.1 = (f32[128]{0:T(128)S(1)}, f32[128]{0:T(128)}, u32[]{:S(2)}) copy-start(f32[128]{0:T(128)} %param.23) | copy-start | bytes 1540
  53.0 19.2 %copy-start.4 = (bf16[1,128,2048]{2,1,0:T(8,128)(2,1)S(1)}, bf16[1,128,2048]{2,1,0:T(8,128)(2,1)}, u32[]{:S(2)}) copy-start(bf16[1,128,2048]{2,1,0:T(8,128)(2,1)} %param.18) | copy-start | bytes 1572868
  53.0 19.2 %copy-start.5 = (bf16[1,128,2048]{2,1,0:T(8,128)(2,1)S(1)}, bf16[1,128,2048]{2,1,0:T(8,128)(2,1)}, u32[]{:S(2)}) copy-start(bf16[1,128,2048]{2,1,0:T(8,128)(2,1)} %param.19) | copy-start | bytes 1572868
  53.1 19.0 %all-to-all-start.1 = ((bf16[8,128,256]{2,1,0:T(8,128)(2,1)}), bf16[8,128,256]{2,1,0:T(8,128)(2,1)S(1)}, u32[]{:S(2)}, u32[]{:S(2)}) async-start(bf16[8,128,256]{2,1,0:T(8,128)(2,1)} %bitcast.35), calls=%async_computation.1 | async-start | bytes 1048576 | tf_op jit(solution)/shard_map/all_to_all | solution.py:731
  72.3 5.0 %copy-start.3 = (f32[2048]{0:T(1024)S(1)}, f32[2048]{0:T(1024)}, u32[]{:S(2)}) copy-start(f32[2048]{0:T(1024)} %param.25) | copy-start | bytes 24580
  77.2 1.0 copy-start.2

commit v4 on v3

--- a/solution.py
+++ b/solution.py
@@ -499,16 +499,18 @@
         for rel, kind in ((1, 2), (3, 5), (5, 6), (7, 7)):
             arrived(feat.at[s, rel], d_send.at[s, kind], d_recv.at[s, kind], beside(1))
 
-    def experts(s, load):
+    def experts(s, load, between=None):
         wide = 512
 
         def choose(n, carry):
             at = pl.ds(pl.multiple_of(n * wide, wide), wide)
-            found = [mm(pick_ref[s, rel], feat[s, rel, :, at]) for rel in range(8)]
-            for j in range(2):
-                routed[j, :, at] = jnp.concatenate(
-                    [f[j * cap : (j + 1) * cap] for f in found], 0
-                ).astype(BF)
+            for pair in range(4):
+                block = feat[s, 2 * pair : 2 * pair + 2, :, at].reshape(2 * tokens, wide)
+                found = mm(pick_ref[s, pair], block).astype(BF)
+                for j in range(2):
+                    routed[j, pair * rows : (pair + 1) * rows, at] = found[
+                        j * rows : (j + 1) * rows
+                    ]
             return carry
 
         lax.fori_loop(0, D // wide, choose, 0)
@@ -526,6 +528,9 @@
                 return carry
 
             lax.fori_loop(0, FF // step, lift, 0)
+
+        if between is not None:
+            between()
 
         def lower(n, carry):
             at = pl.ds(pl.multiple_of(n * wide, wide), wide)
@@ -573,8 +578,6 @@
         def pass_on():
             along(place, place + 1, inward if place == 1 else outward).start()
 
-        spread(d)
-
     own, first, second, third = order
     feat[own, 0] = x_ref[...]
     along(0, 0, inward).start()
@@ -585,16 +588,21 @@
 
     spread(own)
     take(1)
+    spread(first)
     forward(own)
     take(2)
     forward(first)
+    spread(second)
     take(3)
     complete(first)
-    experts(first, True)
-    forward(second)
+
+    def during_first():
+        spread(third)
+        forward(second)
+
+    experts(first, True, during_first)
     complete(second)
-    experts(second, False)
-    forward(third)
+    experts(second, False, lambda: forward(third))
     complete(third)
     experts(third, False)
     combine(first, True)
@@ -622,7 +630,7 @@
 
 def moe(n_dp, expert_input, hidden_state, pick, weight, expert_in, expert_out):
     tokens = expert_input.shape[0]
-    rows = pick.shape[2]
+    rows = pick.shape[2] // 2
     vmem = pl.BlockSpec(memory_space=pltpu.VMEM)
     hbm = pl.BlockSpec(memory_space=pl.ANY)
     dma = pltpu.SemaphoreType.DMA
@@ -742,7 +750,9 @@
     my_gates = lax.dynamic_index_in_dim(my_gates, my_dp, 3, False).transpose(0, 1, 3, 2)
     my_gates = my_gates[:, places]
     pick = slot_table(my_gates, capacity).astype(BF)
-    pick = pick.reshape(n_dp, n_ctx, local * capacity, tokens)
+    pick = pick.reshape(n_dp, n_ctx // 2, 2, local, capacity, tokens).transpose(0, 1, 3, 2, 4, 5)
+    pick = pick[..., None, :] * jnp.eye(2, dtype=BF)[:, None, :, None]
+    pick = pick.reshape(n_dp, n_ctx // 2, local * 2 * capacity, 2 * tokens)
     plane = column_gates.reshape(n_dp, n_dp, n_ctx, local, tokens)
     plane = lax.dynamic_index_in_dim(plane, my_dp, 1, False)[:, places]
     weight = jnp.where(slot_table(plane, capacity), plane[..., None, :], 0)

time: 264 us -> 256 us (0.970)
  Pallas kernels: 203 us -> 187 us
  waiting for transfers between devices: 1.75 us -> 8.76 us
    pallas_call x1, Pallas kernels: 182 us -> 167 us  [moe(): pl.pallas_call(functools.partial(moe_kernel, n_dp), out_shape=jax.ShapeDt...]
    all_to_all x1, waiting for transfers between devices: 0.01 us -> 7.11 us  [per_device(): lax.all_to_all(mixed.reshape(n_ctx, tokens, group * DV), 'ctx', split_axi...]
    unnamed x17 -> x18, local copies, waits for them, and re-layouts: 5.47 us -> 5.49 us
  transfers between devices with their start and end apart: 2 -> 2, of which waited for: 1 -> 2; matrix products, arithmetic and copies ran while one was open for 2% -> 2% of each run, Pallas kernels for 0% -> 0%
where the time goes in v4:
time: 256 us; the launch traced here: 255 us
  Pallas kernels  187 us (73%)
  blocking collectives  26.8 us (10%)
  local copies, waits for them, and re-layouts  11.7 us (5%)
  starting transfers between devices  8.85 us (3%)
  waiting for transfers between devices  8.76 us (3%)
  other arithmetic  6.13 us (2%)
  matrix products  5.2 us (2%)
    pallas_call x1, Pallas kernels, moe(): pl.pallas_call(functools.partial(moe_kernel, n_dp), out_shape=jax.ShapeDt...  167 us
    pallas_call x1, Pallas kernels, mixer(): pl.pallas_call(mixer_kernel, out_shape=jax.ShapeDtypeStruct((total, group...  20.7 us
    all_gather x1, blocking collectives, per_device(): lax.all_gather(heads[:, :, gates_at:gates_at + n_dp * local], 'dp')  13.4 us
    all_gather x1, blocking collectives, per_device(): column_gates = lax.all_gather(gate_table, 'dp')  13.4 us
    all_to_all x1, waiting for transfers between devices, per_device(): lax.all_to_all(mixed.reshape(n_ctx, tokens, group * DV), 'ctx', split_axi...  7.11 us
    unnamed x18, local copies, waits for them, and re-layouts  5.49 us
    all_to_all x1, starting transfers between devices, per_device(): heads = lax.all_to_all(sent, 'ctx', split_axis=0, concat_axis=0, tiled=True)  5.17 us
  transfers between devices with their start and end apart: 2, of which 2 were waited for; matrix products, arithmetic and copies ran while one was open for 2% of the time, Pallas kernels for 0%

profile of v4, /device:TPU:0, one launch (start us, length us, event | category | flops | bytes accessed | tf_op | source)
XLA Modules:
  0.0 255.1 jit_solution(4141011803380495610)
XLA Ops:
  0.0 0.8 slice_bitcast_fusion.19
  0.8 0.8 slice_bitcast_fusion.18
  1.8 0.7 reduce-precision_convert_fusion
  2.5 0.7 reduce-precision_convert_fusion.1
  3.2 1.3 copy.62
  4.6 1.1 copy.60
  5.7 1.1 copy.61
  7.0 1.2 pad_maximum_fusion
  8.2 5.2 %all-to-all-start = ((bf16[8,128,640]{1,2,0:T(8,128)(2,1)}), bf16[8,128,640]{1,2,0:T(8,128)(2,1)S(1)}, u32[]{:S(2)}, u32[]{:S(2)}) async-start(bf16[8,128,640]{1,2,0:T(8,128)(2,1)} %pad_maximum_fusion), calls=%async_computation | async-start | bytes 2621440 | tf_op jit(solution)/shard_map/all_to_all | solution.py:735
  13.5 13.4 %all_gather.12 = bf16[4,64,128]{2,1,0:T(8,128)(2,1)S(1)} all-gather(bf16[1,64,128]{2,1,0:T(8,128)(2,1)S(1)} %add_convert_fusion), channel_id=1, replica_groups=mesh['dp'=4,'ctx'=8] {'dp'}, dimensions={0}, use_global_device_ids=true | all-gather | bytes 81920 | tf_op jit(solution)/shard_map/all_gather | solution.py:719
  26.9 0.6 gather_fusion.1
  28.9 1.0 fusion.14.weight_ref
  29.9 1.6 all-to-all-done
  31.6 13.4 %all-gather = bf16[32,128,8]{1,2,0:T(8,128)(2,1)S(1)} all-gather(bf16[8,128,8]{1,2,0:T(8,128)(2,1)S(1)} %slice.88), channel_id=2, replica_groups=mesh['dp'=4,'ctx'=8] {'dp'}, dimensions={0}, use_global_device_ids=true | all-gather | bytes 81920 | tf_op jit(solution)/shard_map/all_gather | solution.py:737
  45.8 0.7 copy.65
  46.6 20.7 %shard_map.145 = bf16[1024,256]{1,0:T(8,128)(2,1)} custom-call(s32[1,4]{1,0:T(1,128)S(1)} %copy-done, bf16[1024,640]{1,0:T(8,128)(2,1)S(1)} %bitcast.116, f32[1,128]{1,0:T(1,128)S(1)} %bitcast.117), custom_call_target="tpu_custom_call" | custom-call | tf_op jit(solution)/shard_map/pallas_call | solution.py:411
  67.3 3.7 %all-to-all-start.1 = ((bf16[8,128,256]{2,1,0:T(8,128)(2,1)}), bf16[8,128,256]{2,1,0:T(8,128)(2,1)S(1)}, u32[]{:S(2)}, u32[]{:S(2)}) async-start(bf16[8,128,256]{2,1,0:T(8,128)(2,1)} %bitcast.35), calls=%async_computation.1 | async-start | bytes 1048576 | tf_op jit(solution)/shard_map/all_to_all | solution.py:739
  71.2 0.7 mul.53
  72.4 0.9 broadcast_multiply_fusion.pick_ref
  73.4 7.1 %all-to-all-done.1 = bf16[8,128,256]{2,1,0:T(8,128)(2,1)S(1)} async-done(((bf16[8,128,256]{2,1,0:T(8,128)(2,1)}), bf16[8,128,256]{2,1,0:T(8,128)(2,1)S(1)}, u32[]{:S(2)}, u32[]{:S(2)}) %all-to-all-start.1) | async-done | bytes 524320 | tf_op jit(solution)/shard_map/all_to_all | solution.py:739
  80.7 4.9 %fusion.1 = (f32[128]{0:T(128)S(1)}, bf16[128,2048]{1,0:T(8,128)(2,1)S(1)}) fusion(bf16[2048,2048]{1,0:T(8,128)(2,1)} %param.24, f32[128,2048]{1,0:T(8,128)S(1)} %bitcast.124, bf16[1,128,2048]{2,1,0:T(8,128)(2,1)S(1)} %copy-done.4, bf16[1,128,2048]{2,1,0:T(8,128)(2,1)S(1)} %copy-done.5), kind=kOutput, calls=%fused_computation.9 | convolution fusion | flops 1077149568 | bytes 11010560 | tf_op jit(solution)/shard_map/dot_general | solution.py:744
  85.7 1.0 fusion.3.x_ref
  86.7 166.5 %shard_map.146 = bf16[128,2048]{1,0:T(8,128)(2,1)} custom-call(bf16[128,2048]{1,0:T(8,128)(2,1)} %fusion.3.x_ref, bf16[128,2048]{1,0:T(8,128)(2,1)} %copy-done.2, bf16[4,4,96,256]{3,2,1,0:T(8,128)(2,1)} %broadcast_multiply_fusion.pick_ref, bf16[4,128,384]{2,1,0:T(8,128)(2,1)} %fusion.14.weight_ref, bf16[2,2048,1024]{2,1,0:T(8,128)(2,1)} %in_hbm.1, ...), custom_call_target="tpu_custom_call" | custom-call | tf_op jit(solution)/shard_map/pallas_call | solution.py:637
  253.2 1.9 copy.101
  (58 shorter events, 3.6 us)
Async XLA Ops:
  8.2 23.4 %all-to-all-start = ((bf16[8,128,640]{1,2,0:T(8,128)(2,1)}), bf16[8,128,640]{1,2,0:T(8,128)(2,1)S(1)}, u32[]{:S(2)}, u32[]{:S(2)}) async-start(bf16[8,128,640]{1,2,0:T(8,128)(2,1)} %pad_maximum_fusion), calls=%async_computation | async-start | bytes 2621440 | tf_op jit(solution)/shard_map/all_to_all | solution.py:735
  28.4 18.1 %copy-start = (s32[1,4]{1,0:T(1,128)S(1)}, s32[1,4]{1,0:T(1,128)}, u32[]{:S(2)}) copy-start(s32[1,4]{1,0:T(1,128)} %lengths_ref.1) | copy-start | bytes 52
  28.5 18.1 %copy-start.1 = (f32[128]{0:T(128)S(1)}, f32[128]{0:T(128)}, u32[]{:S(2)}) copy-start(f32[128]{0:T(128)} %param.23) | copy-start | bytes 1540
  67.3 13.2 %all-to-all-start.1 = ((bf16[8,128,256]{2,1,0:T(8,128)(2,1)}), bf16[8,128,256]{2,1,0:T(8,128)(2,1)S(1)}, u32[]{:S(2)}, u32[]{:S(2)}) async-start(bf16[8,128,256]{2,1,0:T(8,128)(2,1)} %bitcast.35), calls=%async_computation.1 | async-start | bytes 1048576 | tf_op jit(solution)/shard_map/all_to_all | solution.py:739
  72.4 8.3 %copy-start.4 = (bf16[1,128,2048]{2,1,0:T(8,128)(2,1)S(1)}, bf16[1,128,2048]{2,1,0:T(8,128)(2,1)}, u32[]{:S(2)}) copy-start(bf16[1,128,2048]{2,1,0:T(8,128)(2,1)} %param.18) | copy-start | bytes 1572868
  72.4 8.3 %copy-start.5 = (bf16[1,128,2048]{2,1,0:T(8,128)(2,1)S(1)}, bf16[1,128,2048]{2,1,0:T(8,128)(2,1)}, u32[]{:S(2)}) copy-start(bf16[1,128,2048]{2,1,0:T(8,128)(2,1)} %param.19) | copy-start | bytes 1572868
  80.7 5.0 %copy-start.3 = (f32[2048]{0:T(1024)S(1)}, f32[2048]{0:T(1024)}, u32[]{:S(2)}) copy-start(f32[2048]{0:T(1024)} %param.25) | copy-start | bytes 24580
  85.7 1.0 copy-start.2

commit v5 on v4

--- a/solution.py
+++ b/solution.py
@@ -717,15 +717,12 @@
         )
     gate_table = gate_table.astype(BF)
     column_gates = lax.all_gather(gate_table, "dp")
-    gate_cols = gate_table.reshape(n_dp, n_ctx, local, tokens).transpose(1, 3, 0, 2)
-    gate_cols = gate_cols.reshape(n_ctx, tokens, n_dp * local)
 
     beta = jax.nn.sigmoid(beta_logit[0])
     dh, dl = two_parts(log_decay[0])
     bh, bl = two_parts(beta)
     scal = jnp.stack([dh, dl, bh, bl]).reshape(4, n_ctx, group, tokens)
     scal = scal.transpose(1, 3, 0, 2).reshape(n_ctx, tokens, 4 * group)
-    scal = jnp.concatenate([scal, gate_cols], -1)
     scal = jnp.pad(scal, ((0, 0), (0, 0), (0, SCAL - scal.shape[-1])))
 
     def by_head(a):
@@ -733,12 +730,17 @@
 
     sent = jnp.concatenate([by_head(queries), by_head(key_in), by_head(value_in), scal], -1)
     heads = lax.all_to_all(sent, "ctx", split_axis=0, concat_axis=0, tiled=True)
-    gates_at = 2 * DK + group * DV + 4 * group
-    plane_gates = lax.all_gather(heads[:, :, gates_at : gates_at + n_dp * local], "dp")
     mixed = mixer(lengths, heads.reshape(n_ctx * tokens, -1), head_gain)
-    mine = lax.all_to_all(
-        mixed.reshape(n_ctx, tokens, group * DV), "ctx", split_axis=0, concat_axis=0, tiled=True
-    )
+    plane = column_gates.reshape(n_dp, n_dp, n_ctx, local, tokens)
+    plane = lax.dynamic_index_in_dim(plane, my_dp, 1, False)
+    gate_rows = plane.transpose(1, 0, 2, 3).reshape(n_ctx, -1, group * DV)
+    extra = gate_rows.shape[1]
+    gate_rows = jnp.pad(gate_rows, ((0, 0), (0, -extra % 16), (0, 0)))
+    mixed = jnp.concatenate([mixed.reshape(n_ctx, tokens, group * DV), gate_rows], 1)
+    mine = lax.all_to_all(mixed, "ctx", split_axis=0, concat_axis=0, tiled=True)
+    my_gates = mine[:, tokens : tokens + extra].reshape(n_ctx, n_dp, local, tokens)
+    my_gates = my_gates.transpose(1, 0, 2, 3)
+    mine = mine[:, :tokens]
     unit = mine.transpose(1, 0, 2).reshape(tokens, HV * DV)
     normed = (unit.astype(F32) * jax.nn.silu(gate_in[0].astype(F32))).astype(BF)
     projected = jnp.dot(normed, out_proj, preferred_element_type=F32)
@@ -746,15 +748,12 @@
     expert_input = post_norm(hidden_state, post_gain)
 
     places = my_ctx ^ jnp.arange(n_ctx)
-    my_gates = plane_gates.reshape(n_dp, n_ctx, tokens, n_dp, local)
-    my_gates = lax.dynamic_index_in_dim(my_gates, my_dp, 3, False).transpose(0, 1, 3, 2)
     my_gates = my_gates[:, places]
     pick = slot_table(my_gates, capacity).astype(BF)
     pick = pick.reshape(n_dp, n_ctx // 2, 2, local, capacity, tokens).transpose(0, 1, 3, 2, 4, 5)
     pick = pick[..., None, :] * jnp.eye(2, dtype=BF)[:, None, :, None]
     pick = pick.reshape(n_dp, n_ctx // 2, local * 2 * capacity, 2 * tokens)
-    plane = column_gates.reshape(n_dp, n_dp, n_ctx, local, tokens)
-    plane = lax.dynamic_index_in_dim(plane, my_dp, 1, False)[:, places]
+    plane = plane[:, places]
     weight = jnp.where(slot_table(plane, capacity), plane[..., None, :], 0)
     weight = weight.reshape(n_dp, n_ctx * local * capacity, tokens).transpose(0, 2, 1)
     return moe(n_dp, expert_input, hidden_state, pick, weight, expert_in, expert_out)[None]

time: 256 us -> 244 us (0.953)
  blocking collectives: 26.8 us -> 13.4 us
  waiting for transfers between devices: 8.76 us -> 11.8 us
    all_gather x1 -> x0, blocking collectives: 13.4 us -> none  [per_device(): lax.all_gather(heads[:, :, gates_at:gates_at + n_dp * local], 'dp')]
    unnamed x18 -> x22, local copies, waits for them, and re-layouts: 5.49 us -> 5.73 us
  transfers between devices with their start and end apart: 2 -> 2, of which waited for: 2 -> 2; matrix products, arithmetic and copies ran while one was open for 2% -> 1% of each run, Pallas kernels for 0% -> 0%
where the time goes in v5:
time: 244 us; the launch traced here: 243 us
  Pallas kernels  187 us (77%)
  blocking collectives  13.4 us (5%)
  waiting for transfers between devices  11.8 us (5%)
  local copies, waits for them, and re-layouts  9.67 us (4%)
  starting transfers between devices  8.89 us (4%)
  other arithmetic  6.95 us (3%)
  matrix products  5.23 us (2%)
    pallas_call x1, Pallas kernels, moe(): pl.pallas_call(functools.partial(moe_kernel, n_dp), out_shape=jax.ShapeDt...  167 us
    pallas_call x1, Pallas kernels, mixer(): pl.pallas_call(mixer_kernel, out_shape=jax.ShapeDtypeStruct((total, group...  20 us
    all_gather x1, blocking collectives, per_device(): column_gates = lax.all_gather(gate_table, 'dp')  13.4 us
    all_to_all x1, waiting for transfers between devices, per_device(): mine = lax.all_to_all(mixed, 'ctx', split_axis=0, concat_axis=0, tiled=True)  7.87 us
    unnamed x22, local copies, waits for them, and re-layouts  5.73 us
    all_to_all x1, starting transfers between devices, per_device(): heads = lax.all_to_all(sent, 'ctx', split_axis=0, concat_axis=0, tiled=True)  5.17 us
    dot_general x1, matrix products, per_device(): projected = jnp.dot(normed, out_proj, preferred_element_type=F32)  4.96 us
  transfers between devices with their start and end apart: 2, of which 2 were waited for; matrix products, arithmetic and copies ran while one was open for 1% of the time, Pallas kernels for 0%

profile of v5, /device:TPU:0, one launch (start us, length us, event | category | flops | bytes accessed | tf_op | source)
XLA Modules:
  0.0 243.1 jit_solution(8060615557657740342)
XLA Ops:
  0.0 0.7 reduce-precision_convert_fusion.1
  0.7 0.7 reduce-precision_convert_fusion
  1.7 1.0 copy.82
  2.7 1.0 copy.83
  3.7 1.2 copy.84
  5.1 1.2 fusion.2
  6.3 5.2 %all-to-all-start = ((bf16[8,128,640]{2,1,0:T(8,128)(2,1)}), bf16[8,128,640]{2,1,0:T(8,128)(2,1)S(1)}, u32[]{:S(2)}, u32[]{:S(2)}) async-start(bf16[8,128,640]{2,1,0:T(8,128)(2,1)} %fusion.2), calls=%async_computation | async-start | bytes 2621440 | tf_op jit(solution)/shard_map/all_to_all | solution.py:732
  11.6 13.4 %all_gather.4 = bf16[4,64,128]{2,1,0:T(8,128)(2,1)S(1)} all-gather(bf16[1,64,128]{2,1,0:T(8,128)(2,1)S(1)} %add_convert_fusion), channel_id=1, replica_groups=mesh['dp'=4,'ctx'=8] {'dp'}, dimensions={0}, use_global_device_ids=true | all-gather | bytes 81920 | tf_op jit(solution)/shard_map/all_gather | solution.py:719
  25.1 0.6 gather_fusion.1
  25.7 3.9 %all-to-all-done = bf16[8,128,640]{2,1,0:T(8,128)(2,1)S(1)} async-done(((bf16[8,128,640]{2,1,0:T(8,128)(2,1)}), bf16[8,128,640]{2,1,0:T(8,128)(2,1)S(1)}, u32[]{:S(2)}, u32[]{:S(2)}) %all-to-all-start) | async-done | bytes 1310752 | tf_op jit(solution)/shard_map/all_to_all | solution.py:732
  29.7 20.0 %shard_map.145 = bf16[1024,256]{1,0:T(8,128)(2,1)S(1)} custom-call(s32[1,4]{1,0:T(1,128)S(1)} %copy-done, bf16[1024,640]{1,0:T(8,128)(2,1)S(1)} %bitcast.126, f32[1,128]{1,0:T(1,128)S(1)} %bitcast.128), custom_call_target="tpu_custom_call" | custom-call | tf_op jit(solution)/shard_map/pallas_call | solution.py:411
  49.7 0.9 fusion.12
  50.5 3.7 %all-to-all-start.1 = ((bf16[8,144,256]{2,1,0:T(8,128)(2,1)}), bf16[8,144,256]{2,1,0:T(8,128)(2,1)S(1)}, u32[]{:S(2)}, u32[]{:S(2)}) async-start(bf16[8,144,256]{2,1,0:T(8,128)(2,1)} %fusion.12), calls=%async_computation.1 | async-start | bytes 1179648 | tf_op jit(solution)/shard_map/all_to_all | solution.py:740
  55.1 0.3 copy.73
  55.6 1.0 fusion.16.weight_ref
  56.6 7.9 %all-to-all-done.1 = bf16[8,144,256]{2,1,0:T(8,128)(2,1)S(1)} async-done(((bf16[8,144,256]{2,1,0:T(8,128)(2,1)}), bf16[8,144,256]{2,1,0:T(8,128)(2,1)S(1)}, u32[]{:S(2)}, u32[]{:S(2)}) %all-to-all-start.1) | async-done | bytes 589856 | tf_op jit(solution)/shard_map/all_to_all | solution.py:740
  64.4 0.6 gather_fusion
  65.5 0.7 mul.53
  66.2 0.5 mul.54
  67.4 5.0 %fusion.4 = (f32[128]{0:T(128)S(1)}, bf16[128,2048]{1,0:T(8,128)(2,1)S(1)}) fusion(bf16[2048,2048]{1,0:T(8,128)(2,1)} %param.24, f32[128,2048]{1,0:T(8,128)S(1)} %bitcast.134, bf16[1,128,2048]{2,1,0:T(8,128)(2,1)S(1)} %copy-done.6, bf16[1,128,2048]{2,1,0:T(8,128)(2,1)S(1)} %copy-done.7), kind=kOutput, calls=%fused_computation.13 | convolution fusion | flops 1077149568 | bytes 11010560 | tf_op jit(solution)/shard_map/dot_general | solution.py:746
  72.3 1.0 broadcast_multiply_fusion.pick_ref
  73.4 1.0 fusion.6.x_ref
  74.4 166.8 %shard_map.146 = bf16[128,2048]{1,0:T(8,128)(2,1)} custom-call(bf16[128,2048]{1,0:T(8,128)(2,1)} %fusion.6.x_ref, bf16[128,2048]{1,0:T(8,128)(2,1)} %copy-done.2, bf16[4,4,96,256]{3,2,1,0:T(8,128)(2,1)} %broadcast_multiply_fusion.pick_ref, bf16[4,128,384]{2,1,0:T(8,128)(2,1)} %fusion.16.weight_ref, bf16[2,2048,1024]{2,1,0:T(8,128)(2,1)} %in_hbm.1, ...), custom_call_target="tpu_custom_call" | custom-call | tf_op jit(solution)/shard_map/pallas_call | solution.py:637
  241.2 1.9 copy.100
  (53 shorter events, 2.7 us)
Async XLA Ops:
  5.0 6.4 %copy-start.4 = (s32[1,128,10]{1,0,2:T(1,128)S(1)}, s32[1,128,10]{1,0,2:T(1,128)}, u32[]{:S(2)}) copy-start(s32[1,128,10]{1,0,2:T(1,128)} %param.28) | copy-start | bytes 15364
  5.0 6.5 %copy-start.5 = (f32[1,128,10]{1,0,2:T(1,128)S(1)}, f32[1,128,10]{1,0,2:T(1,128)}, u32[]{:S(2)}) copy-start(f32[1,128,10]{1,0,2:T(1,128)} %param.29) | copy-start | bytes 15364
  5.1 24.6 %copy-start = (s32[1,4]{1,0:T(1,128)S(1)}, s32[1,4]{1,0:T(1,128)}, u32[]{:S(2)}) copy-start(s32[1,4]{1,0:T(1,128)} %lengths_ref.1) | copy-start | bytes 52
  5.1 24.6 %copy-start.1 = (f32[128]{0:T(128)S(1)}, f32[128]{0:T(128)}, u32[]{:S(2)}) copy-start(f32[128]{0:T(128)} %param.23) | copy-start | bytes 1540
  6.3 23.4 %all-to-all-start = ((bf16[8,128,640]{2,1,0:T(8,128)(2,1)}), bf16[8,128,640]{2,1,0:T(8,128)(2,1)S(1)}, u32[]{:S(2)}, u32[]{:S(2)}) async-start(bf16[8,128,640]{2,1,0:T(8,128)(2,1)} %fusion.2), calls=%async_computation | async-start | bytes 2621440 | tf_op jit(solution)/shard_map/all_to_all | solution.py:732
  50.5 13.9 %all-to-all-start.1 = ((bf16[8,144,256]{2,1,0:T(8,128)(2,1)}), bf16[8,144,256]{2,1,0:T(8,128)(2,1)S(1)}, u32[]{:S(2)}, u32[]{:S(2)}) async-start(bf16[8,144,256]{2,1,0:T(8,128)(2,1)} %fusion.12), calls=%async_computation.1 | async-start | bytes 1179648 | tf_op jit(solution)/shard_map/all_to_all | solution.py:740
  66.1 1.0 copy-start.6
  66.2 1.2 copy-start.7
  67.3 6.0 %copy-start.3 = (f32[2048]{0:T(1024)S(1)}, f32[2048]{0:T(1024)}, u32[]{:S(2)}) copy-start(f32[2048]{0:T(1024)} %param.25) | copy-start | bytes 24580
  72.3 2.1 copy-start.2
